TPU v7x, 32 devices: a whole 2x2x4 slice. The times are simulated.
32 devices in a mesh: seq: 16 (over z, x, core), wshard: 2 (over y).
Axes of the slice: x: 2, y: 2, z: 4, core: 2. Of those that a mesh axis runs over, the one named last changes fastest.
Arguments:
- hidden: bfloat16 [8, 2048, 1024], P('wshard', 'seq'), may hold values from -6 to 6
- segments: int32 [8, 2048], P('wshard', 'seq'), may hold values from 0 to 2, never falling along the last dimension, each value on 1 to 1536 neighbouring positions
- cotangent: bfloat16 [8, 2048, 1024], P('wshard', 'seq'), may hold values from -6 to 6
- in_weight: bfloat16 [1024, 3, 1024], P(None, None, 'wshard'), may hold values from -0.1875 to 0.1875
- out_weight: bfloat16 [1024, 1024], P('wshard'), may hold values from -0.1875 to 0.1875
- gate_weight: bfloat16 [1024, 4608], P(None, 'wshard'), may hold values from -0.1875 to 0.1875
- up_weight: bfloat16 [1024, 4608], P(None, 'wshard'), may hold values from -0.1875 to 0.1875
- down_weight: bfloat16 [4608, 1024], P('wshard'), may hold values from -0.09375 to 0.09375
- conv_weight: bfloat16 [3, 1024], P(None, 'wshard'), may hold values from -3 to 3
- norm_mix: bfloat16 [1024], P('wshard'), may hold values from 0.5 to 1.5
- norm_ffn: bfloat16 [1024], P('wshard'), may hold values from 0.5 to 1.5
Outputs:
- block_out: bfloat16 [8, 2048, 1024], P('wshard', 'seq')
- grad_hidden: float32 [8, 2048, 1024], P('wshard', 'seq')
- grad_in: float32 [1024, 3, 1024], P('seq', None, 'wshard')
- grad_out: float32 [1024, 1024], P('wshard', 'seq')
- grad_gate: float32 [1024, 4608], P('seq', 'wshard')
- grad_up: float32 [1024, 4608], P('seq', 'wshard')
- grad_down: float32 [4608, 1024], P('wshard', 'seq')
- grad_conv: float32 [3, 1024], P(None, 'wshard')
- grad_norm_mix: float32 [1024], P('wshard')
- grad_norm_ffn: float32 [1024], P('wshard')
Inputs may be any that keep to these rules, and one draw needn't show every extreme that they name: `segments`: segment numbers never fall along a sequence; each document holds 1 to 1536 tokens, one exactly that many.
All inputs are finite; a program needn't handle non-finite values.
Results may differ from a plain program's by a relative error of at most 0.017.
Values may be sent and summed in bfloat16 or wider, within the bound.
No kernel may reach another device: no remote copies, remote signals or barrier semaphores. Data moves between devices by JAX's collectives and lax.ppermute only.
A program may use at most 256 MiB of HBM per device.

v0:
```python
import jax
import jax.numpy as jnp
from jax import lax
from jax.sharding import PartitionSpec as P

EPS = 1e-05
LOW = jnp.bfloat16
F32 = jnp.float32


def over_seq(block, route):
    return lax.ppermute(block, "seq", route)


def swap_seq(block, mask):
    return over_seq(block, [(i, i ^ mask) for i in range(lax.axis_size("seq"))])


def swap_core(block):
    return swap_seq(block, 1)


def swap_pair(block):
    return lax.ppermute(block, "wshard", [(0, 1), (1, 0)])


def swap(block, link):
    return swap_pair(block) if link == "pair" else swap_seq(block, 2 * link)


def mm(left, right):
    return jnp.dot(left, right, preferred_element_type=F32)


def mm_tn(left, right):
    return lax.dot_general(left, right, (((0,), (0,)), ((), ())), preferred_element_type=F32)


def mm_nt(left, right):
    return lax.dot_general(left, right, (((1,), (1,)), ((), ())), preferred_element_type=F32)


def norm_stats(values):
    return lax.rsqrt(jnp.mean(values * values, axis=-1, keepdims=True) + EPS)


def norm_back(upstream, values, scale, gain):
    scaled = values * scale
    weighted = upstream * gain
    inner = jnp.mean(weighted * scaled, axis=-1, keepdims=True)
    return scale * (weighted - scaled * inner)


def slot_masks(order):
    masks = [0]
    for link in reversed(order):
        masks = masks + [mask ^ link for mask in masks]
    return masks


def in_slots(grad, chip, order):
    chips = lax.axis_size("seq") // 2
    blocks = grad.astype(LOW).reshape(chips, grad.shape[0] // chips, grad.shape[1])
    return jnp.stack(
        [lax.dynamic_index_in_dim(blocks, chip ^ mask, 0, False) for mask in slot_masks(order)]
    )


def halving(send, keep, order):
    terms = [keep]
    half = keep.shape[0]
    terms.append(swap(send, order[0]))
    for link in order[1:]:
        half //= 2
        going = sum((term[half : 2 * half].astype(F32) for term in terms)).astype(LOW)
        terms.append(swap(going, link))
    return sum((term[0].astype(F32) for term in terms))


def scatter_seq(grad, chip, order):
    slots = in_slots(grad, chip, order)
    half = slots.shape[0] // 2
    return halving(slots[half:], slots[:half], order)


def scatter_all(mine, other, chip, order):
    return halving(in_slots(other, chip, order[1:]), in_slots(mine, chip, order[1:]), order)


def local(
    hidden,
    segments,
    cotangent,
    in_weight,
    out_weight,
    gate_weight,
    up_weight,
    down_weight,
    conv_weight,
    norm_mix,
    norm_ffn,
):
    groups, block, width = hidden.shape
    rows = groups * block
    size = lax.axis_size("seq")
    seq_index = lax.axis_index("seq")
    core = seq_index % 2
    chip = seq_index // 2
    pair = lax.axis_index("wshard")
    first_core = core == 0
    chips = size // 2
    links = [1 << bit for bit in range(chips.bit_length() - 1)]
    features = out_weight.shape[0] // 2
    units = gate_weight.shape[1] // 2

    def ordered(flag, mine, other, axis):
        return jnp.where(
            flag,
            jnp.concatenate([mine, other], axis=axis),
            jnp.concatenate([other, mine], axis=axis),
        )

    small = jnp.concatenate([conv_weight, norm_mix[None], norm_ffn[None]], axis=0)
    small_other = swap_pair(small)
    gains = ordered(pair == 0, small[3:], small_other[3:], 1).astype(F32)
    gain_mix, gain_ffn = (gains[0], gains[1])

    def of_core(array, axis):
        return lax.dynamic_slice_in_dim(
            array, core * (array.shape[axis] // 2), array.shape[axis] // 2, axis
        )

    taps = jnp.concatenate([of_core(small[:3], 1), of_core(small_other[:3], 1)], axis=1).astype(F32)
    in_mine = of_core(jnp.transpose(in_weight, (1, 0, 2)), 2)
    in_other = swap_pair(in_mine)
    out_mine = of_core(out_weight, 0)
    out_other = swap_pair(out_mine)
    in_mat = jnp.concatenate([part for j in range(3) for part in (in_mine[j], in_other[j])], axis=1)
    out_mat = jnp.concatenate([out_mine, out_other], axis=0)
    conv_width = 2 * features
    own = hidden.reshape(rows, width)
    chip_hidden = jnp.concatenate([own, swap_core(own)], axis=0)
    seg_low = segments.astype(LOW)
    seg_other = swap_core(segments)
    edge = jnp.concatenate(
        [hidden, jnp.broadcast_to(seg_low[:, :, None], (groups, block, 128))], axis=2
    )
    last, head = (edge[:, block - 2 :], edge[:, :2])
    odd = range(1, size - 1, 2)
    even = range(2, size, 2)
    before = jnp.where(
        first_core,
        over_seq(last, [(i, i + 1) for i in odd]),
        over_seq(last, [(i, i + 2) for i in odd]),
    )
    after = jnp.where(
        first_core,
        over_seq(head, [(i, i - 2) for i in even]),
        over_seq(head, [(i, i - 1) for i in even]),
    )
    edges = jnp.concatenate([before, after], axis=0)
    edge_hidden = edges[:, :, :width].reshape(4 * groups, width)
    edge_segs = edges[:, :, width].astype(jnp.int32)
    resid = chip_hidden.astype(F32)
    scale_mix = norm_stats(resid)
    normed_mix = (resid * scale_mix * gain_mix).astype(LOW)
    edge_resid = edge_hidden.astype(F32)
    edge_normed = (edge_resid * norm_stats(edge_resid) * gain_mix).astype(LOW)
    projected = mm(normed_mix, in_mat)
    edge_projected = mm(edge_normed, in_mat)
    b_part = projected[:, :conv_width]
    c_part = projected[:, conv_width : 2 * conv_width]
    x_part = projected[:, 2 * conv_width :]

    def by_core(array):
        return array.reshape((2, groups, block) + array.shape[1:])

    def lead(own_lead, other_lead):
        return jnp.stack([own_lead, other_lead])

    conv_in = by_core((b_part * x_part).astype(LOW).astype(F32))
    edge_conv_in = (
        (edge_projected[: 2 * groups, :conv_width] * edge_projected[: 2 * groups, 2 * conv_width :])
        .astype(LOW)
        .astype(F32)
        .reshape(groups, 2, conv_width)
    )
    edge_c = edge_projected[2 * groups :, conv_width : 2 * conv_width]
    segs = jnp.stack([segments, seg_other])
    segs_before, segs_after = (edge_segs[:groups], edge_segs[groups:])

    def with_before(values, outside):
        ahead = jnp.where(
            first_core,
            lead(outside, values[0, :, block - 2 :]),
            lead(values[1, :, block - 2 :], outside),
        )
        return jnp.concatenate([ahead, values], axis=2)

    def with_after(values, outside):
        behind = jnp.where(
            first_core, lead(values[1, :, :2], outside), lead(outside, values[0, :, :2])
        )
        return jnp.concatenate([values, behind], axis=2)

    ext = with_before(conv_in, edge_conv_in)
    segs_ext = with_before(segs, segs_before)
    keep_one = (segs_ext[:, :, 1 : 1 + block] == segs).astype(F32)[..., None]
    keep_two = (segs_ext[:, :, :block] == segs).astype(F32)[..., None]
    lag_one = keep_one * ext[:, :, 1 : 1 + block]
    lag_two = keep_two * ext[:, :, :block]
    conv_out = (taps[2] * conv_in + taps[1] * lag_one + taps[0] * lag_two).reshape(
        2 * rows, conv_width
    )
    mixed = (c_part * conv_out).astype(LOW)
    mix_part = mm(mixed, out_mat).astype(LOW)
    mix_other = swap_core(mix_part)
    mix_term = mix_part.astype(F32) + jnp.concatenate(
        [mix_other[rows:], mix_other[:rows]], axis=0
    ).astype(F32)
    resid_two = resid + mix_term
    scale_ffn = norm_stats(resid_two)
    normed_ffn = (resid_two * scale_ffn * gain_ffn).astype(LOW)

    def gathered(mine):
        far = swap_pair(mine)
        return (far, swap_core(far))

    cot = cotangent.reshape(rows, width)
    cot_chip = jnp.concatenate([cot, swap_core(cot)], axis=0)
    cot_far = jnp.concatenate(gathered(cot), axis=0)
    normed_far = jnp.concatenate(gathered(normed_ffn[:rows]), axis=0)
    gate_mat = of_core(gate_weight, 1)
    up_mat = of_core(up_weight, 1)
    down_mat = of_core(down_weight, 0)

    def feed_forward(normed, upstream):
        gate = mm(normed, gate_mat)
        up_value = mm(normed, up_mat)
        d_act = mm_nt(upstream, down_mat)
        sigma = jax.nn.sigmoid(gate)
        silu_gate = gate * sigma
        act = (silu_gate * up_value).astype(LOW)
        d_gate = (d_act * up_value * sigma * (1.0 + gate * (1.0 - sigma))).astype(LOW)
        d_up = (d_act * silu_gate).astype(LOW)
        term = mm(act, down_mat).astype(LOW)
        d_normed = (mm_nt(d_gate, gate_mat) + mm_nt(d_up, up_mat)).astype(LOW)
        return (act, d_gate, d_up, term, d_normed)

    near_out = feed_forward(normed_ffn, cot_chip)
    far_out = feed_forward(normed_far, cot_far)

    def home(near, far):
        near_sum = near[:rows].astype(F32) + swap_core(near[rows:]).astype(F32)
        far_sum = (far[:rows].astype(F32) + swap_core(far[rows:]).astype(F32)).astype(LOW)
        return near_sum + swap_pair(far_sum).astype(F32)

    d_normed_ffn = home(near_out[4], far_out[4])
    block_out = (resid_two[:rows] + home(near_out[3], far_out[3])).astype(LOW)
    all_normed = jnp.concatenate([normed_ffn, normed_far], axis=0)
    all_cot = jnp.concatenate([cot_chip, cot_far], axis=0)
    act, d_gate, d_up = (jnp.concatenate([near_out[i], far_out[i]], axis=0) for i in range(3))
    part_down = scatter_seq(mm_tn(all_cot, act), chip, links)
    part_gate = scatter_seq(mm_tn(all_normed, d_gate), chip, links)
    part_up = scatter_seq(mm_tn(all_normed, d_up), chip, links)
    upstream = cot.astype(F32)
    own_two, own_scale = (resid_two[:rows], scale_ffn[:rows])
    d_resid_two = upstream + norm_back(d_normed_ffn, own_two, own_scale, gain_ffn)
    grad_gain_ffn = jnp.sum(d_normed_ffn * own_two * own_scale, axis=0)
    d_resid_low = d_resid_two.astype(LOW)
    d_chip = jnp.concatenate([d_resid_low, swap_core(d_resid_low)], axis=0)
    d_head = d_resid_low.reshape(groups, block, width)[:, :2]
    d_after = jnp.where(
        first_core,
        over_seq(d_head, [(i, i - 2) for i in even]),
        over_seq(d_head, [(i, i - 1) for i in even]),
    ).reshape(2 * groups, width)
    d_mixed = mm_nt(d_chip, out_mat)
    edge_d_conv = (mm_nt(d_after, out_mat) * edge_c).reshape(groups, 2, conv_width)
    d_conv = by_core(d_mixed * c_part)
    d_c = d_mixed * conv_out
    grad_taps = jnp.stack(
        [
            jnp.sum(d_conv * lag_two, axis=(0, 1, 2)),
            jnp.sum(d_conv * lag_one, axis=(0, 1, 2)),
            jnp.sum(d_conv * conv_in, axis=(0, 1, 2)),
        ]
    )
    d_ext = with_after(d_conv, edge_d_conv)
    segs_next = with_after(segs, segs_after)
    next_one = (segs_next[:, :, 1 : 1 + block] == segs).astype(F32)[..., None]
    next_two = (segs_next[:, :, 2 : 2 + block] == segs).astype(F32)[..., None]
    d_conv_in = (
        taps[2] * d_conv
        + taps[1] * next_one * d_ext[:, :, 1 : 1 + block]
        + taps[0] * next_two * d_ext[:, :, 2 : 2 + block]
    ).reshape(2 * rows, conv_width)
    d_proj = jnp.concatenate([d_conv_in * x_part, d_c, d_conv_in * b_part], axis=1).astype(LOW)
    grad_out = mm_tn(d_chip, mixed)
    grad_in = mm_tn(normed_mix, d_proj)
    d_normed_part = mm_nt(d_proj, in_mat).astype(LOW)
    d_normed_mix = d_normed_part[:rows].astype(F32) + swap_core(d_normed_part[rows:]).astype(F32)
    own_resid, own_mix = (resid[:rows], scale_mix[:rows])
    grad_hidden = (d_resid_two + norm_back(d_normed_mix, own_resid, own_mix, gain_mix)).reshape(
        groups, block, width
    )
    grad_gain_mix = jnp.sum(d_normed_mix * own_resid * own_mix, axis=0)
    halves = [grad_out] + [grad_in[:, j * conv_width : (j + 1) * conv_width] for j in range(3)]
    mixed_mine = jnp.concatenate([half[:, :features] for half in halves], axis=1)
    mixed_far = jnp.concatenate([half[:, features:] for half in halves], axis=1)
    part_mix = scatter_all(mixed_mine, mixed_far, chip, ["pair"] + links)
    part_rows = width // size

    def finish(part):
        low = part.astype(LOW).reshape(2, part_rows, -1)
        came = swap_core(lax.dynamic_index_in_dim(low, 1 - core, 0, False)).astype(F32)
        mine = lax.dynamic_index_in_dim(part.reshape(2, part_rows, -1), core, 0, False)
        return (mine, came)

    def wide(part):
        mine, came = finish(part)
        return ordered(first_core, mine, came, 1)

    out_down = wide(part_down).T
    out_gate = wide(part_gate)
    out_up = wide(part_up)
    mix_mine, mix_came = finish(part_mix)
    mix_parts = [
        ordered(
            first_core,
            mix_mine[:, j * features : (j + 1) * features],
            mix_came[:, j * features : (j + 1) * features],
            1,
        )
        for j in range(4)
    ]
    out_out = mix_parts[0].T
    out_in = jnp.stack(mix_parts[1:], axis=1)
    half_width = norm_mix.shape[0]
    spread = jnp.zeros((3, width), F32)
    spread = lax.dynamic_update_slice_in_dim(
        spread, grad_taps[:, :features], pair * half_width + core * features, 1
    )
    spread = lax.dynamic_update_slice_in_dim(
        spread, grad_taps[:, features:], (1 - pair) * half_width + core * features, 1
    )
    sums = lax.psum(
        jnp.concatenate([spread, grad_gain_mix[None], grad_gain_ffn[None]], axis=0),
        ("seq", "wshard"),
    )
    sums = lax.dynamic_slice_in_dim(sums, pair * half_width, half_width, 1)
    return (
        block_out.reshape(groups, block, width),
        grad_hidden,
        out_in,
        out_out,
        out_gate,
        out_up,
        out_down,
        sums[:3],
        sums[3],
        sums[4],
    )


def solution(mesh):
    return jax.shard_map(
        local,
        mesh=mesh,
        in_specs=(
            P("wshard", "seq", None),
            P("wshard", "seq"),
            P("wshard", "seq", None),
            P(None, None, "wshard"),
            P("wshard", None),
            P(None, "wshard"),
            P(None, "wshard"),
            P("wshard", None),
            P(None, "wshard"),
            P("wshard"),
            P("wshard"),
        ),
        out_specs=(
            P("wshard", "seq", None),
            P("wshard", "seq", None),
            P("seq", None, "wshard"),
            P("wshard", "seq"),
            P("seq", "wshard"),
            P("seq", "wshard"),
            P("wshard", "seq"),
            P(None, "wshard"),
            P("wshard"),
            P("wshard"),
        ),
        check_vma=False,
    )
```

profile of v0, /device:TPU:0, one launch (start us, length us, event | category | flops | bytes accessed | tf_op | source)
XLA Modules:
  0.0 517.6 jit_solution(11000948463357092600)
XLA Ops:
  0.7 3.2 copy.56
  9.0 3.0 collective-permute-start.2
  12.7 4.7 collective-permute-start.7
  17.4 1.9 fusion.80
  19.3 1.9 constant_dynamic-slice_fusion.25
  21.6 25.2 %collective-permute-done.1 = bf16[5,512]{1,0:T(8,128)(2,1)S(1)} collective-permute-done((bf16[5,512]{1,0:T(8,128)(2,1)S(1)}, bf16[5,512]{1,0:T(8,128)(2,1)S(1)}, u32[]{:S(2)}, u32[]{:S(2)}) %collective-permute-start.1) | collective-permute-done | bytes 5152 | tf_op jit(solution)/shard_map/ppermute | solution.py:24
  51.0 1.9 fusion.79
  52.9 2.0 fusion.78
  54.8 2.0 fusion.77
  56.8 1.9 fusion.76
  58.7 1.9 fusion.75
  60.6 2.4 fusion.86
  63.7 5.4 %fusion.73 = f32[1024,1536]{1,0:T(8,128)S(1)} fusion(bf16[1024,1536]{1,0:T(8,128)(2,1)} %fusion.75, f32[1024]{0:T(1024)S(1)} %bitcast.190, f32[1024]{0:T(1024)S(1)} %add_rsqrt_fusion.1, bf16[512,1024]{1,0:T(8,128)(2,1)S(1)} %collective-permute-done, bf16[512,1024]{1,0:T(8,128)(2,1)S(1)} %bitcast.148), kind=kOutput, calls=%fused_computation.131 | convolution fusion | flops 3228565504 | bytes 11542528 | tf_op jit(solution)/shard_map/dot_general | solution.py:32
  73.1 4.2 convolution_convert_fusion.4
  77.5 1.5 collective-permute-start.17
  79.7 23.4 %collective-permute-done.17 = bf16[512,1024]{1,0:T(8,128)(2,1)} collective-permute-done((bf16[512,1024]{1,0:T(8,128)(2,1)}, bf16[512,1024]{1,0:T(8,128)(2,1)}, u32[]{:S(2)}, u32[]{:S(2)}) %collective-permute-start.17) | collective-permute-done | bytes 1048608 | tf_op jit(solution)/shard_map/ppermute | solution.py:24
  103.1 3.6 fusion.121
  106.8 1.9 fusion.125
  108.7 2.7 multiply_reduce_fusion
  111.9 1.6 collective-permute-start.11
  113.5 4.5 fusion.61
  118.0 4.5 fusion.69
  122.6 9.7 %multiply_convert_fusion.2 = (bf16[1024,1152]{1,0:T(8,128)(2,1)S(1)}, bf16[1024,1152]{1,0:T(8,128)(2,1)}, bf16[1024,1152]{1,0:T(8,128)(2,1)}) fusion(f32[1024,1152]{1,0:T(8,128)} %fusion.69, f32[1024,1152]{1,0:T(8,128)} %fusion.61, bf16[2304,1024]{1,0:T(8,128)(2,1)S(1)} %bitcast.220, s32[]{:T(128)S(6)} %select_n.227, ...), kind=kOutput, calls=%fused_computation.14 | convolution fusion | flops 2437808128 | bytes 20971524 | tf_op jit(solution)/shard_map/dot_general | solution.py:40
  132.3 6.1 %fusion.65 = f32[1024,1024]{1,0:T(8,128)S(1)} fusion(bf16[1024,1152]{1,0:T(8,128)(2,1)} %get-tuple-element.24, bf16[1024,2304]{1,0:T(8,128)(2,1)} %param.16, s32[]{:T(128)S(6)} %select_n.227), kind=kOutput, calls=%fused_computation.113 | convolution fusion | flops 2415919104 | bytes 8912900 | tf_op jit(solution)/shard_map/dot_general | solution.py:40
  138.8 5.0 add_convert_fusion.1
  145.1 3.3 convolution_convert_fusion.2
  149.6 4.5 fusion.59
  154.1 4.5 fusion.67
  158.6 11.4 %multiply_convert_fusion = (bf16[1024,1152]{1,0:T(8,128)(2,1)S(1)}, bf16[1024,1152]{1,0:T(8,128)(2,1)}, bf16[1024,1152]{1,0:T(8,128)(2,1)}) fusion(f32[1024,1152]{1,0:T(8,128)} %fusion.67, f32[1024,1152]{1,0:T(8,128)} %fusion.59, bf16[2304,1024]{1,0:T(8,128)(2,1)} %param.18, s32[]{:T(128)S(6)} %select_n.227, bf16[512,1024]{1,0:T(8,128)(2,1)} %collective-permute-done.18, ...), kind=kOutput, calls=%fused_computation.12 | convolution fusion | flops 2437808128 | bytes 20971524 | tf_op jit(solution)/shard_map/dot_general | solution.py:40
  170.1 6.1 %convolution_convert_fusion.1 = bf16[1024,1024]{1,0:T(8,128)(2,1)S(1)} fusion(bf16[1024,1152]{1,0:T(8,128)(2,1)} %get-tuple-element.28, bf16[2304,1024]{1,0:T(8,128)(2,1)} %param.18, s32[]{:T(128)S(6)} %select_n.227), kind=kOutput, calls=%fused_computation.96 | convolution fusion | flops 2416967680 | bytes 6815748 | tf_op jit(solution)/shard_map/dot_general | solution.py:32
  177.6 4.6 fusion.63
  182.2 3.6 add_convert_fusion
  187.7 9.3 %fusion.21 = bf16[1024,1152]{1,0:T(8,128)(2,1)S(1)} fusion(bf16[1024,1152]{1,0:T(8,128)(2,1)} %get-tuple-element.28, bf16[1024,1152]{1,0:T(8,128)(2,1)} %get-tuple-element.25, bf16[512,1024]{1,0:T(8,128)(2,1)} %collective-permute-done.18, bf16[512,1024]{1,0:T(8,128)(2,1)} %collective-permute-done.17, bf16[512,1024]{1,0:T(8,128)(2,1)} %collective-permute-done.15, ...), kind=kOutput, calls=%fused_computation.37 | convolution fusion | flops 4859232256 | bytes 11272192 | tf_op jit(solution)/shard_map/dot_general | solution.py:36
  198.4 1.5 collective-permute-start.38
  199.9 8.2 %fusion.26 = bf16[1024,1152]{1,0:T(8,128)(2,1)S(1)} fusion(bf16[1024,1152]{1,0:T(8,128)(2,1)} %copy-done.38, bf16[1024,1152]{1,0:T(8,128)(2,1)} %copy-done.37, bf16[512,1024]{1,0:T(8,128)(2,1)S(1)} %collective-permute-done.12, bf16[512,1024]{1,0:T(8,128)(2,1)S(1)} %collective-permute-done.11, bf16[1024,1024]{1,0:T(8,128)(2,1)S(1)} %multiply_convert_fusion.6), kind=kOutput, calls=%fused_computation.38 | convolution fusion | flops 4855037952 | bytes 11272192 | tf_op jit(solution)/shard_map/dot_general | solution.py:36
  210.2 8.8 %fusion.29 = bf16[1024,1152]{1,0:T(8,128)(2,1)S(1)} fusion(bf16[1024,1152]{1,0:T(8,128)(2,1)} %get-tuple-element.27, bf16[1024,1152]{1,0:T(8,128)(2,1)} %get-tuple-element.24, bf16[512,1024]{1,0:T(8,128)(2,1)} %copy-done.24, bf16[512,1024]{1,0:T(8,128)(2,1)} %copy-done.23, bf16[1024,1024]{1,0:T(8,128)(2,1)S(1)} %multiply_convert_fusion.6), kind=kOutput, calls=%fused_computation.39 | convolution fusion | flops 4855037952 | bytes 11272192 | tf_op jit(solution)/shard_map/dot_general | solution.py:36
  220.9 1.6 add_convert_fusion.5
  222.5 1.5 collective-permute-start.30
  224.1 1.6 add_convert_fusion.3
  225.7 1.8 collective-permute-done.38
  229.3 23.5 %collective-permute-done.34 = bf16[4,128,1152]{2,1,0:T(8,128)(2,1)} collective-permute-done((bf16[4,128,1152]{2,1,0:T(8,128)(2,1)}, bf16[4,128,1152]{2,1,0:T(8,128)(2,1)}, u32[]{:S(2)}, u32[]{:S(2)}) %collective-permute-start.34) | collective-permute-done | bytes 1179680 | tf_op jit(solution)/shard_map/ppermute | solution.py:12
  252.8 1.6 collective-permute-start.39
  255.6 21.7 %collective-permute-done.30 = bf16[4,128,1152]{2,1,0:T(8,128)(2,1)S(1)} collective-permute-done((bf16[4,128,1152]{2,1,0:T(8,128)(2,1)S(1)}, bf16[4,128,1152]{2,1,0:T(8,128)(2,1)S(1)}, u32[]{:S(2)}, u32[]{:S(2)}) %collective-permute-start.30) | collective-permute-done | bytes 1179680 | tf_op jit(solution)/shard_map/ppermute | solution.py:12
  277.3 1.6 collective-permute-start.35
  280.6 12.9 %collective-permute-done.35 = bf16[2,128,1152]{2,1,0:T(8,128)(2,1)S(1)} collective-permute-done((bf16[2,128,1152]{2,1,0:T(8,128)(2,1)S(1)}, bf16[2,128,1152]{2,1,0:T(8,128)(2,1)S(1)}, u32[]{:S(2)}, u32[]{:S(2)}) %collective-permute-start.35) | collective-permute-done | bytes 589856 | tf_op jit(solution)/shard_map/ppermute | solution.py:12
  295.3 9.3 %collective-permute-done.31 = bf16[2,128,1152]{2,1,0:T(8,128)(2,1)S(1)} collective-permute-done((bf16[2,128,1152]{2,1,0:T(8,128)(2,1)S(1)}, bf16[2,128,1152]{2,1,0:T(8,128)(2,1)S(1)}, u32[]{:S(2)}, u32[]{:S(2)}) %collective-permute-start.31) | collective-permute-done | bytes 589856 | tf_op jit(solution)/shard_map/ppermute | solution.py:12
  304.6 2.6 collective-permute-start.40
  307.3 11.9 %collective-permute-done.40 = bf16[1,128,1152]{2,1,0:T(8,128)(2,1)S(1)} collective-permute-done((bf16[1,128,1152]{2,1,0:T(8,128)(2,1)S(1)}, bf16[1,128,1152]{2,1,0:T(8,128)(2,1)S(1)}, u32[]{:S(2)}, u32[]{:S(2)}) %collective-permute-start.40) | collective-permute-done | bytes 294944 | tf_op jit(solution)/shard_map/ppermute | solution.py:12
  320.3 14.0 %collective-permute-done.36 = bf16[1,128,1152]{2,1,0:T(8,128)(2,1)S(1)} collective-permute-done((bf16[1,128,1152]{2,1,0:T(8,128)(2,1)S(1)}, bf16[1,128,1152]{2,1,0:T(8,128)(2,1)S(1)}, u32[]{:S(2)}, u32[]{:S(2)}) %collective-permute-start.36) | collective-permute-done | bytes 294944 | tf_op jit(solution)/shard_map/ppermute | solution.py:12
  336.9 11.6 %collective-permute-done.32 = bf16[1,128,1152]{2,1,0:T(8,128)(2,1)S(1)} collective-permute-done((bf16[1,128,1152]{2,1,0:T(8,128)(2,1)S(1)}, bf16[1,128,1152]{2,1,0:T(8,128)(2,1)S(1)}, u32[]{:S(2)}, u32[]{:S(2)}) %collective-permute-start.32) | collective-permute-done | bytes 294944 | tf_op jit(solution)/shard_map/ppermute | solution.py:12
  349.6 4.0 fusion.122
  359.1 2.5 collective-permute-done.22
  361.6 1.6 convolution_multiply_fusion
  366.2 4.6 multiply_reduce_fusion.6
  374.0 2.9 convolution_convert_fusion.5
  377.0 3.7 convolution_convert_fusion
  384.8 3.7 convolution_convert_fusion.3
  389.9 40.0 %collective-permute-done.25 = bf16[8,128,1024]{2,1,0:T(8,128)(2,1)S(1)} collective-permute-done((bf16[8,128,1024]{2,1,0:T(8,128)(2,1)S(1)}, bf16[8,128,1024]{2,1,0:T(8,128)(2,1)S(1)}, u32[]{:S(2)}, u32[]{:S(2)}) %collective-permute-start.25) | collective-permute-done | bytes 2097184 | tf_op jit(solution)/shard_map/ppermute | solution.py:24
  430.3 3.0 collective-permute-start.26
  435.1 21.7 %collective-permute-done.26 = bf16[4,128,1024]{2,1,0:T(8,128)(2,1)S(1)} collective-permute-done((bf16[4,128,1024]{2,1,0:T(8,128)(2,1)S(1)}, bf16[4,128,1024]{2,1,0:T(8,128)(2,1)S(1)}, u32[]{:S(2)}, u32[]{:S(2)}) %collective-permute-start.26) | collective-permute-done | bytes 1048608 | tf_op jit(solution)/shard_map/ppermute | solution.py:12
  457.3 2.0 multiply_add_fusion
  459.2 11.3 %collective-permute-done.27 = bf16[2,128,1024]{2,1,0:T(8,128)(2,1)S(1)} collective-permute-done((bf16[2,128,1024]{2,1,0:T(8,128)(2,1)S(1)}, bf16[2,128,1024]{2,1,0:T(8,128)(2,1)S(1)}, u32[]{:S(2)}, u32[]{:S(2)}) %collective-permute-start.27) | collective-permute-done | bytes 524320 | tf_op jit(solution)/shard_map/ppermute | solution.py:12
  471.4 40.1 %psum.7 = f32[5,1024]{1,0:T(8,128)S(1)} all-reduce(f32[5,1024]{1,0:T(8,128)S(1)} %pad_maximum_fusion.23), channel_id=1, replica_groups=mesh['seq'=16,'wshard'=2] {'seq','wshard'}, use_global_device_ids=true, to_apply=%region_10.11 | all-reduce | flops 5120 | bytes 40960 | tf_op jit(solution)/shard_map/psum | solution.py:347
  512.7 1.5 convert_add_fusion.5
  (310 shorter events, 63.9 us)
Async XLA Ops:
  0.6 7.1 %copy-start = (bf16[1024,3,512]{2,0,1:T(8,128)(2,1)S(1)}, bf16[1024,3,512]{2,0,1:T(8,128)(2,1)}, u32[]{:S(2)}) copy-start(bf16[1024,3,512]{2,0,1:T(8,128)(2,1)} %param.14) | copy-start | bytes 9437188
  3.8 8.8 %copy-start.34 = (s32[4,128]{1,0:T(4,128)S(1)}, s32[4,128]{1,0:T(4,128)}, u32[]{:S(2)}) copy-start(s32[4,128]{1,0:T(4,128)} %param.12) | copy-start | bytes 6148
  5.7 13.6 %copy-start.35 = (bf16[512]{0:T(512)(128)(2,1)S(1)}, bf16[512]{0:T(512)(128)(2,1)}, u32[]{:S(2)}) copy-start(bf16[512]{0:T(512)(128)(2,1)} %param.20) | copy-start | bytes 3076
  5.7 13.6 %copy-start.36 = (bf16[512]{0:T(512)(128)(2,1)S(1)}, bf16[512]{0:T(512)(128)(2,1)}, u32[]{:S(2)}) copy-start(bf16[512]{0:T(512)(128)(2,1)} %param.21) | copy-start | bytes 3076
  5.7 41.8 %collective-permute-start.5 = (bf16[4,2,1152]{2,0,1:T(4,128)(2,1)S(1)}, bf16[4,2,1152]{2,0,1:T(4,128)(2,1)S(1)}, u32[]{:S(2)}, u32[]{:S(2)}) collective-permute-start(bf16[4,2,1152]{2,0,1:T(4,128)(2,1)S(1)} %get-tuple-element.69), channel_id=1, source_target_pairs={{4,0},{8,4},{12,8},{16,12},{20,16},{24,20},{28,24},{5,1},{9,5},{13... | collective-permute-start | bytes 55304 | tf_op jit(solution)/shard_map/ppermute | solution.py:12
  7.0 41.0 %collective-permute-start.6 = (bf16[4,2,1152]{2,0,1:T(4,128)(2,1)S(1)}, bf16[4,2,1152]{2,0,1:T(4,128)(2,1)S(1)}, u32[]{:S(2)}, u32[]{:S(2)}) collective-permute-start(bf16[4,2,1152]{2,0,1:T(4,128)(2,1)S(1)} %get-tuple-element.69), channel_id=1, source_target_pairs={{4,2},{8,6},{12,10},{16,14},{20,18},{24,22},{28,26},{5,3},{9,7},{1... | collective-permute-start | bytes 55304 | tf_op jit(solution)/shard_map/ppermute | solution.py:12
  7.7 13.5 %copy-start.33 = (bf16[3,512]{1,0:T(4,128)(2,1)S(1)}, bf16[3,512]{1,0:T(4,128)(2,1)}, u32[]{:S(2)}) copy-start(bf16[3,512]{1,0:T(4,128)(2,1)} %param.19) | copy-start | bytes 9220
  9.0 38.6 %copy-start.6 = (bf16[4,128,1024]{2,1,0:T(8,128)(2,1)S(1)}, bf16[4,128,1024]{2,1,0:T(8,128)(2,1)}, u32[]{:S(2)}) copy-start(bf16[4,128,1024]{2,1,0:T(8,128)(2,1)} %param.11) | copy-start | bytes 3145732
  9.0 42.0 %collective-permute-start.2 = (bf16[3,1024,256]{2,1,0:T(8,128)(2,1)}, bf16[3,1024,256]{2,1,0:T(8,128)(2,1)}, u32[]{:S(2)}, u32[]{:S(2)}) collective-permute-start(bf16[3,1024,256]{2,1,0:T(8,128)(2,1)} %dynamic-slice_bitcast_fusion), channel_id=1, source_target_pairs={{0,1},{1,0},{2,3},{3,2},{4,5},{5,4},{6,7},{7,6},{8,9},{9,8},{10,11... | collective-permute-start | bytes 4718600 | tf_op jit(solution)/shard_map/ppermute | solution.py:24
  11.9 37.5 %collective-permute-start.3 = (bf16[4,2,1152]{2,0,1:T(4,128)(2,1)S(1)}, bf16[4,2,1152]{2,0,1:T(4,128)(2,1)S(1)}, u32[]{:S(2)}, u32[]{:S(2)}) collective-permute-start(bf16[4,2,1152]{2,0,1:T(4,128)(2,1)S(1)} %get-tuple-element.68), channel_id=1, source_target_pairs={{2,4},{6,8},{10,12},{14,16},{18,20},{22,24},{26,28},{3,5},{7,9},{1... | collective-permute-start | bytes 55304 | tf_op jit(solution)/shard_map/ppermute | solution.py:12
  12.7 8.6 %collective-permute-start.7 = (s32[4,128]{0,1:T(8,128)S(1)}, s32[4,128]{0,1:T(8,128)S(1)}, u32[]{:S(2)}, u32[]{:S(2)}) collective-permute-start(s32[4,128]{0,1:T(8,128)S(1)} %copy.57), channel_id=1, source_target_pairs={{0,2},{2,0},{4,6},{6,4},{8,10},{10,8},{12,14},{14,12},{16,18},{18,... | collective-permute-start | bytes 6152 | tf_op jit(solution)/shard_map/ppermute | solution.py:12
  21.3 25.4 %collective-permute-start.1 = (bf16[5,512]{1,0:T(8,128)(2,1)S(1)}, bf16[5,512]{1,0:T(8,128)(2,1)S(1)}, u32[]{:S(2)}, u32[]{:S(2)}) collective-permute-start(bf16[5,512]{1,0:T(8,128)(2,1)S(1)} %pad_maximum_fusion.26), channel_id=1, source_target_pairs={{0,1},{1,0},{2,3},{3,2},{4,5},{5,4},{6,7},{7,6},{8,9},{9,8},{10,11... | collective-permute-start | bytes 15368 | tf_op jit(solution)/shard_map/ppermute | solution.py:24
  46.7 2.7 collective-permute-start.4
  47.4 15.7 %copy-start.28 = (f32[1,1024]{1,0:T(1,128)}, f32[1,1024]{1,0:T(1,128)S(1)}, u32[]{:S(2)}) copy-start(f32[1,1024]{1,0:T(1,128)S(1)} %get-tuple-element.90) | copy-start | bytes 12292
  47.5 2.9 collective-permute-start
  48.0 25.1 %collective-permute-start.8 = (bf16[256,1024]{1,0:T(8,128)(2,1)}, bf16[256,1024]{1,0:T(8,128)(2,1)}, u32[]{:S(2)}, u32[]{:S(2)}) collective-permute-start(bf16[256,1024]{1,0:T(8,128)(2,1)} %constant_dynamic-slice_fusion.25), channel_id=1, source_target_pairs={{0,1},{1,0},{2,3},{3,2},{4,5},{5,4},{6,7},{7,6},{8,9},{9,8},{10,11... | collective-permute-start | bytes 1572872 | tf_op jit(solution)/shard_map/ppermute | solution.py:24
  50.4 12.7 %copy-start.7 = (bf16[512,1024]{1,0:T(8,128)(2,1)}, bf16[512,1024]{1,0:T(8,128)(2,1)S(1)}, u32[]{:S(2)}) copy-start(bf16[512,1024]{1,0:T(8,128)(2,1)S(1)} %collective-permute-done) | copy-start | bytes 3145732
  50.9 28.2 %copy-start.31 = (f32[1024]{0:T(1024)}, f32[1024]{0:T(1024)S(1)}, u32[]{:S(2)}) copy-start(f32[1024]{0:T(1024)S(1)} %add_rsqrt_fusion.1) | copy-start | bytes 12292
  77.2 29.5 %collective-permute-start.9 = (bf16[1024,1024]{1,0:T(8,128)(2,1)}, bf16[1024,1024]{1,0:T(8,128)(2,1)}, u32[]{:S(2)}, u32[]{:S(2)}) collective-permute-start(bf16[1024,1024]{1,0:T(8,128)(2,1)} %convolution_convert_fusion.4), channel_id=1, source_target_pairs={{0,2},{2,0},{4,6},{6,4},{8,10},{10,8},{12,14},{14,12},{16,18},{18,... | collective-permute-start | bytes 6291464 | tf_op jit(solution)/shard_map/ppermute | solution.py:12
  77.5 25.7 %collective-permute-start.17 = (bf16[512,1024]{1,0:T(8,128)(2,1)}, bf16[512,1024]{1,0:T(8,128)(2,1)}, u32[]{:S(2)}, u32[]{:S(2)}) collective-permute-start(bf16[512,1024]{1,0:T(8,128)(2,1)} %bitcast.18), channel_id=1, source_target_pairs={{0,1},{1,0},{2,3},{3,2},{4,5},{5,4},{6,7},{7,6},{8,9},{9,8},{10,11... | collective-permute-start | bytes 3145736 | tf_op jit(solution)/shard_map/ppermute | solution.py:24
  78.9 43.6 %collective-permute-start.15 = (bf16[512,1024]{1,0:T(8,128)(2,1)}, bf16[512,1024]{1,0:T(8,128)(2,1)}, u32[]{:S(2)}, u32[]{:S(2)}) collective-permute-start(bf16[512,1024]{1,0:T(8,128)(2,1)} %bitcast.18), channel_id=1, source_target_pairs={{0,2},{2,0},{4,6},{6,4},{8,10},{10,8},{12,14},{14,12},{16,18},{18,... | collective-permute-start | bytes 3145736 | tf_op jit(solution)/shard_map/ppermute | solution.py:12
  103.1 55.5 %collective-permute-start.18 = (bf16[512,1024]{1,0:T(8,128)(2,1)}, bf16[512,1024]{1,0:T(8,128)(2,1)}, u32[]{:S(2)}, u32[]{:S(2)}) collective-permute-start(bf16[512,1024]{1,0:T(8,128)(2,1)} %collective-permute-done.17), channel_id=1, source_target_pairs={{0,2},{2,0},{4,6},{6,4},{8,10},{10,8},{12,14},{14,12},{16,18},{18,... | collective-permute-start | bytes 3145736 | tf_op jit(solution)/shard_map/ppermute | solution.py:12
  106.8 6.8 %slice-start.8 = ((s8[4718592]{0:T(1024)(128)(4,1)}), s8[4194304]{0:T(1024)(128)(4,1)S(1)}, s32[]{:S(2)}) async-start(s8[4718592]{0:T(1024)(128)(4,1)} %bitcast.225), calls=%async_computation.8 | async-start | bytes 8388608
  111.9 26.5 %collective-permute-start.11 = (bf16[512,1024]{1,0:T(8,128)(2,1)S(1)}, bf16[512,1024]{1,0:T(8,128)(2,1)S(1)}, u32[]{:S(2)}, u32[]{:S(2)}) collective-permute-start(bf16[512,1024]{1,0:T(8,128)(2,1)S(1)} %slice.503), channel_id=1, source_target_pairs={{0,1},{1,0},{2,3},{3,2},{4,5},{5,4},{6,7},{7,6},{8,9},{9,8},{10,11... | collective-permute-start | bytes 3145736 | tf_op jit(solution)/shard_map/ppermute | solution.py:24
  113.5 9.0 %slice-start.2 = ((s8[4718592]{0:T(1024)(128)(4,1)}), s8[4194304]{0:T(1024)(128)(4,1)S(1)}, s32[]{:S(2)}) async-start(s8[4718592]{0:T(1024)(128)(4,1)} %bitcast.219), calls=%async_computation.2 | async-start | bytes 8388608
  138.4 61.4 %copy-start.23 = (bf16[512,1024]{1,0:T(8,128)(2,1)}, bf16[512,1024]{1,0:T(8,128)(2,1)S(1)}, u32[]{:S(2)}) copy-start(bf16[512,1024]{1,0:T(8,128)(2,1)S(1)} %collective-permute-done.11) | copy-start | bytes 3145732
  138.4 11.1 %collective-permute-start.12 = (bf16[512,1024]{1,0:T(8,128)(2,1)S(1)}, bf16[512,1024]{1,0:T(8,128)(2,1)S(1)}, u32[]{:S(2)}, u32[]{:S(2)}) collective-permute-start(bf16[512,1024]{1,0:T(8,128)(2,1)S(1)} %collective-permute-done.11), channel_id=1, source_target_pairs={{0,2},{2,0},{4,6},{6,4},{8,10},{10,8},{12,14},{14,12},{16,18},{18,... | collective-permute-start | bytes 3145736 | tf_op jit(solution)/shard_map/ppermute | solution.py:12
  138.8 10.9 %slice-start.10 = ((s8[4718592]{0:T(1024)(128)(4,1)}), s8[524288]{0:T(1024)(128)(4,1)S(1)}, s32[]{:S(2)}) async-start(s8[4718592]{0:T(1024)(128)(4,1)} %bitcast.227), calls=%async_computation.10 | async-start | bytes 1048576
  144.8 203.8 %collective-permute-start.16 = (bf16[512,1024]{1,0:T(8,128)(2,1)}, bf16[512,1024]{1,0:T(8,128)(2,1)S(1)}, u32[]{:S(2)}, u32[]{:S(2)}) collective-permute-start(bf16[512,1024]{1,0:T(8,128)(2,1)} %slice.507), channel_id=1, source_target_pairs={{0,2},{2,0},{4,6},{6,4},{8,10},{10,8},{12,14},{14,12},{16,18},{18,... | collective-permute-start | bytes 3145736 | tf_op jit(solution)/shard_map/ppermute | solution.py:12
  149.5 50.4 %copy-start.24 = (bf16[512,1024]{1,0:T(8,128)(2,1)}, bf16[512,1024]{1,0:T(8,128)(2,1)S(1)}, u32[]{:S(2)}) copy-start(bf16[512,1024]{1,0:T(8,128)(2,1)S(1)} %collective-permute-done.12) | copy-start | bytes 3145732
  170.1 12.0 %copy-start.38 = (bf16[1024,1152]{1,0:T(8,128)(2,1)}, bf16[1024,1152]{1,0:T(8,128)(2,1)S(1)}, u32[]{:S(2)}) copy-start(bf16[1024,1152]{1,0:T(8,128)(2,1)S(1)} %get-tuple-element.26) | copy-start | bytes 7077892
  170.1 7.5 %copy-start.39 = (bf16[1024,1152]{1,0:T(8,128)(2,1)S(1)}, bf16[1024,1152]{1,0:T(8,128)(2,1)}, u32[]{:S(2)}) copy-start(bf16[1024,1152]{1,0:T(8,128)(2,1)} %get-tuple-element.27) | copy-start | bytes 7077892
  170.1 12.1 %slice-start.12 = ((s8[4718592]{0:T(1024)(128)(4,1)}), s8[4194304]{0:T(1024)(128)(4,1)S(1)}, s32[]{:S(2)}) async-start(s8[4718592]{0:T(1024)(128)(4,1)} %bitcast.229), calls=%async_computation.12 | async-start | bytes 8388608
  177.3 42.1 %collective-permute-start.13 = (bf16[512,1024]{1,0:T(8,128)(2,1)}, bf16[512,1024]{1,0:T(8,128)(2,1)}, u32[]{:S(2)}, u32[]{:S(2)}) collective-permute-start(bf16[512,1024]{1,0:T(8,128)(2,1)} %slice.505), channel_id=1, source_target_pairs={{0,2},{2,0},{4,6},{6,4},{8,10},{10,8},{12,14},{14,12},{16,18},{18,... | collective-permute-start | bytes 3145736 | tf_op jit(solution)/shard_map/ppermute | solution.py:12
  187.4 35.1 %collective-permute-start.19 = (bf16[512,1024]{1,0:T(8,128)(2,1)}, bf16[512,1024]{1,0:T(8,128)(2,1)}, u32[]{:S(2)}, u32[]{:S(2)}) collective-permute-start(bf16[512,1024]{1,0:T(8,128)(2,1)} %slice.509), channel_id=1, source_target_pairs={{0,2},{2,0},{4,6},{6,4},{8,10},{10,8},{12,14},{14,12},{16,18},{18,... | collective-permute-start | bytes 3145736 | tf_op jit(solution)/shard_map/ppermute | solution.py:12
  198.4 29.1 %collective-permute-start.38 = (bf16[4,128,1152]{2,1,0:T(8,128)(2,1)}, bf16[4,128,1152]{2,1,0:T(8,128)(2,1)}, u32[]{:S(2)}, u32[]{:S(2)}) collective-permute-start(bf16[4,128,1152]{2,1,0:T(8,128)(2,1)} %pad_maximum_fusion.16), channel_id=1, source_target_pairs={{0,4},{2,6},{4,0},{6,2},{8,12},{10,14},{12,8},{14,10},{16,20},{18,... | collective-permute-start | bytes 3538952 | tf_op jit(solution)/shard_map/ppermute | solution.py:12
  209.7 43.1 %collective-permute-start.34 = (bf16[4,128,1152]{2,1,0:T(8,128)(2,1)}, bf16[4,128,1152]{2,1,0:T(8,128)(2,1)}, u32[]{:S(2)}, u32[]{:S(2)}) collective-permute-start(bf16[4,128,1152]{2,1,0:T(8,128)(2,1)} %pad_maximum_fusion.15), channel_id=1, source_target_pairs={{0,4},{2,6},{4,0},{6,2},{8,12},{10,14},{12,8},{14,10},{16,20},{18,... | collective-permute-start | bytes 3538952 | tf_op jit(solution)/shard_map/ppermute | solution.py:12
  220.2 129.4 %collective-permute-start.10 = (bf16[512,1024]{1,0:T(8,128)(2,1)S(1)}, bf16[512,1024]{1,0:T(8,128)(2,1)S(1)}, u32[]{:S(2)}, u32[]{:S(2)}) collective-permute-start(bf16[512,1024]{1,0:T(8,128)(2,1)S(1)} %copy-done.22), channel_id=1, source_target_pairs={{0,2},{2,0},{4,6},{6,4},{8,10},{10,8},{12,14},{14,12},{16,18},{18,... | collective-permute-start | bytes 3145736 | tf_op jit(solution)/shard_map/ppermute | solution.py:12
  222.5 54.8 %collective-permute-start.30 = (bf16[4,128,1152]{2,1,0:T(8,128)(2,1)S(1)}, bf16[4,128,1152]{2,1,0:T(8,128)(2,1)S(1)}, u32[]{:S(2)}, u32[]{:S(2)}) collective-permute-start(bf16[4,128,1152]{2,1,0:T(8,128)(2,1)S(1)} %pad_maximum_fusion.14), channel_id=1, source_target_pairs={{0,4},{2,6},{4,0},{6,2},{8,12},{10,14},{12,8},{14,10},{16,20},{18,... | collective-permute-start | bytes 3538952 | tf_op jit(solution)/shard_map/ppermute | solution.py:12
  227.5 122.1 %collective-permute-start.14 = (bf16[512,1024]{1,0:T(8,128)(2,1)S(1)}, bf16[512,1024]{1,0:T(8,128)(2,1)S(1)}, u32[]{:S(2)}, u32[]{:S(2)}) collective-permute-start(bf16[512,1024]{1,0:T(8,128)(2,1)S(1)} %add_convert_fusion.5), channel_id=1, source_target_pairs={{0,1},{1,0},{2,3},{3,2},{4,5},{5,4},{6,7},{7,6},{8,9},{9,8},{10,11... | collective-permute-start | bytes 3145736 | tf_op jit(solution)/shard_map/ppermute | solution.py:24
  252.8 26.2 %collective-permute-start.39 = (bf16[2,128,1152]{2,1,0:T(8,128)(2,1)S(1)}, bf16[2,128,1152]{2,1,0:T(8,128)(2,1)S(1)}, u32[]{:S(2)}, u32[]{:S(2)}) collective-permute-start(bf16[2,128,1152]{2,1,0:T(8,128)(2,1)S(1)} %add_convert_fusion.6), channel_id=1, source_target_pairs={{0,8},{2,10},{4,12},{6,14},{8,0},{10,2},{12,4},{14,6},{16,24},{18,... | collective-permute-start | bytes 1769480 | tf_op jit(solution)/shard_map/ppermute | solution.py:12
  277.3 16.3 %collective-permute-start.35 = (bf16[2,128,1152]{2,1,0:T(8,128)(2,1)S(1)}, bf16[2,128,1152]{2,1,0:T(8,128)(2,1)S(1)}, u32[]{:S(2)}, u32[]{:S(2)}) collective-permute-start(bf16[2,128,1152]{2,1,0:T(8,128)(2,1)S(1)} %add_convert_fusion.7), channel_id=1, source_target_pairs={{0,8},{2,10},{4,12},{6,14},{8,0},{10,2},{12,4},{14,6},{16,24},{18,... | collective-permute-start | bytes 1769480 | tf_op jit(solution)/shard_map/ppermute | solution.py:12
  279.0 25.6 %collective-permute-start.31 = (bf16[2,128,1152]{2,1,0:T(8,128)(2,1)S(1)}, bf16[2,128,1152]{2,1,0:T(8,128)(2,1)S(1)}, u32[]{:S(2)}, u32[]{:S(2)}) collective-permute-start(bf16[2,128,1152]{2,1,0:T(8,128)(2,1)S(1)} %add_convert_fusion.8), channel_id=1, source_target_pairs={{0,8},{2,10},{4,12},{6,14},{8,0},{10,2},{12,4},{14,6},{16,24},{18,... | collective-permute-start | bytes 1769480 | tf_op jit(solution)/shard_map/ppermute | solution.py:12
  293.6 55.1 %collective-permute-start.20 = (bf16[512,1024]{1,0:T(8,128)(2,1)S(1)}, bf16[512,1024]{1,0:T(8,128)(2,1)S(1)}, u32[]{:S(2)}, u32[]{:S(2)}) collective-permute-start(bf16[512,1024]{1,0:T(8,128)(2,1)S(1)} %add_convert_fusion.3), channel_id=1, source_target_pairs={{0,1},{1,0},{2,3},{3,2},{4,5},{5,4},{6,7},{7,6},{8,9},{9,8},{10,11... | collective-permute-start | bytes 3145736 | tf_op jit(solution)/shard_map/ppermute | solution.py:24
  304.6 14.6 %collective-permute-start.40 = (bf16[1,128,1152]{2,1,0:T(8,128)(2,1)S(1)}, bf16[1,128,1152]{2,1,0:T(8,128)(2,1)S(1)}, u32[]{:S(2)}, u32[]{:S(2)}) collective-permute-start(bf16[1,128,1152]{2,1,0:T(8,128)(2,1)S(1)} %add_convert_fusion.10), channel_id=1, source_target_pairs={{0,16},{2,18},{4,20},{6,22},{8,24},{10,26},{12,28},{14,30},{16,0},... | collective-permute-start | bytes 884744 | tf_op jit(solution)/shard_map/ppermute | solution.py:12
  319.2 15.1 %collective-permute-start.36 = (bf16[1,128,1152]{2,1,0:T(8,128)(2,1)S(1)}, bf16[1,128,1152]{2,1,0:T(8,128)(2,1)S(1)}, u32[]{:S(2)}, u32[]{:S(2)}) collective-permute-start(bf16[1,128,1152]{2,1,0:T(8,128)(2,1)S(1)} %add_convert_fusion.11), channel_id=1, source_target_pairs={{0,16},{2,18},{4,20},{6,22},{8,24},{10,26},{12,28},{14,30},{16,0},... | collective-permute-start | bytes 884744 | tf_op jit(solution)/shard_map/ppermute | solution.py:12
  334.3 14.2 %collective-permute-start.32 = (bf16[1,128,1152]{2,1,0:T(8,128)(2,1)S(1)}, bf16[1,128,1152]{2,1,0:T(8,128)(2,1)S(1)}, u32[]{:S(2)}, u32[]{:S(2)}) collective-permute-start(bf16[1,128,1152]{2,1,0:T(8,128)(2,1)S(1)} %add_convert_fusion.12), channel_id=1, source_target_pairs={{0,16},{2,18},{4,20},{6,22},{8,24},{10,26},{12,28},{14,30},{16,0},... | collective-permute-start | bytes 884744 | tf_op jit(solution)/shard_map/ppermute | solution.py:12
  353.6 12.6 %collective-permute-start.21 = (bf16[512,1024]{1,0:T(8,128)(2,1)}, bf16[512,1024]{1,0:T(8,128)(2,1)}, u32[]{:S(2)}, u32[]{:S(2)}) collective-permute-start(bf16[512,1024]{1,0:T(8,128)(2,1)} %get-tuple-element.19), channel_id=1, source_target_pairs={{0,2},{2,0},{4,6},{6,4},{8,10},{10,8},{12,14},{14,12},{16,18},{18,... | collective-permute-start | bytes 3145736 | tf_op jit(solution)/shard_map/ppermute | solution.py:12
  355.9 5.7 %collective-permute-start.22 = (bf16[4,2,1024]{2,1,0:T(2,128)(2,1)S(1)}, bf16[4,2,1024]{2,1,0:T(2,128)(2,1)S(1)}, u32[]{:S(2)}, u32[]{:S(2)}) collective-permute-start(bf16[4,2,1024]{2,1,0:T(2,128)(2,1)S(1)} %slice.515), channel_id=1, source_target_pairs={{4,0},{8,4},{12,8},{16,12},{20,16},{24,20},{28,24},{5,1},{9,5},{13... | collective-permute-start | bytes 49160 | tf_op jit(solution)/shard_map/ppermute | solution.py:12
  357.2 4.4 collective-permute-start.23
  358.5 4.7 collective-permute-start.41
  359.1 5.1 collective-permute-start.37
  361.6 3.5 collective-permute-start.33
  365.1 7.6 %slice-start = ((s8[6291456]{0:T(1024)(128)(4,1)}), s8[4194304]{0:T(1024)(128)(4,1)S(1)}, s32[]{:S(2)}) async-start(s8[6291456]{0:T(1024)(128)(4,1)} %bitcast.139), calls=%async_computation | async-start | bytes 8388608
  381.5 48.4 %collective-permute-start.25 = (bf16[8,128,1024]{2,1,0:T(8,128)(2,1)S(1)}, bf16[8,128,1024]{2,1,0:T(8,128)(2,1)S(1)}, u32[]{:S(2)}, u32[]{:S(2)}) collective-permute-start(bf16[8,128,1024]{2,1,0:T(8,128)(2,1)S(1)} %dynamic-slice_dynamic-update-slice_fusion), channel_id=1, source_target_pairs={{0,1},{1,0},{2,3},{3,2},{4,5},{5,4},{6,7},{7,6},{8,9},{9,8},{10,11... | collective-permute-start | bytes 6291464 | tf_op jit(solution)/shard_map/ppermute | solution.py:24
  388.5 45.7 %collective-permute-start.24 = (bf16[512,1024]{1,0:T(8,128)(2,1)S(1)}, bf16[512,1024]{1,0:T(8,128)(2,1)S(1)}, u32[]{:S(2)}, u32[]{:S(2)}) collective-permute-start(bf16[512,1024]{1,0:T(8,128)(2,1)S(1)} %slice.522), channel_id=1, source_target_pairs={{0,2},{2,0},{4,6},{6,4},{8,10},{10,8},{12,14},{14,12},{16,18},{18,... | collective-permute-start | bytes 3145736 | tf_op jit(solution)/shard_map/ppermute | solution.py:12
  389.7 80.8 %copy-start.11 = (bf16[8,128,1024]{2,1,0:T(8,128)(2,1)}, bf16[8,128,1024]{2,1,0:T(8,128)(2,1)S(1)}, u32[]{:S(2)}) copy-start(bf16[8,128,1024]{2,1,0:T(8,128)(2,1)S(1)} %pad_maximum_fusion.6) | copy-start | bytes 6291460
  429.9 40.7 %copy-start.17 = (bf16[8,128,1024]{2,1,0:T(8,128)(2,1)}, bf16[8,128,1024]{2,1,0:T(8,128)(2,1)S(1)}, u32[]{:S(2)}) copy-start(bf16[8,128,1024]{2,1,0:T(8,128)(2,1)S(1)} %collective-permute-done.25) | copy-start | bytes 6291460
  430.3 26.4 %collective-permute-start.26 = (bf16[4,128,1024]{2,1,0:T(8,128)(2,1)S(1)}, bf16[4,128,1024]{2,1,0:T(8,128)(2,1)S(1)}, u32[]{:S(2)}, u32[]{:S(2)}) collective-permute-start(bf16[4,128,1024]{2,1,0:T(8,128)(2,1)S(1)} %add_convert_fusion.2), channel_id=1, source_target_pairs={{0,4},{2,6},{4,0},{6,2},{8,12},{10,14},{12,8},{14,10},{16,20},{18,... | collective-permute-start | bytes 3145736 | tf_op jit(solution)/shard_map/ppermute | solution.py:12
  434.3 23.0 %copy-start.10 = (f32[512,1024]{1,0:T(8,128)S(1)}, f32[512,1024]{1,0:T(8,128)}, u32[]{:S(2)}) copy-start(f32[512,1024]{1,0:T(8,128)} %get-tuple-element.20) | copy-start | bytes 6291460
  456.7 13.8 %copy-start.25 = (bf16[4,128,1024]{2,1,0:T(8,128)(2,1)}, bf16[4,128,1024]{2,1,0:T(8,128)(2,1)S(1)}, u32[]{:S(2)}) copy-start(bf16[4,128,1024]{2,1,0:T(8,128)(2,1)S(1)} %collective-permute-done.26) | copy-start | bytes 3145732
  457.0 13.5 %collective-permute-start.27 = (bf16[2,128,1024]{2,1,0:T(8,128)(2,1)S(1)}, bf16[2,128,1024]{2,1,0:T(8,128)(2,1)S(1)}, u32[]{:S(2)}, u32[]{:S(2)}) collective-permute-start(bf16[2,128,1024]{2,1,0:T(8,128)(2,1)S(1)} %add_convert_fusion.9), channel_id=1, source_target_pairs={{0,8},{2,10},{4,12},{6,14},{8,0},{10,2},{12,4},{14,6},{16,24},{18,... | collective-permute-start | bytes 1572872 | tf_op jit(solution)/shard_map/ppermute | solution.py:12
  471.3 41.4 %collective-permute-start.28 = (bf16[1,128,1024]{2,1,0:T(8,128)(2,1)S(1)}, bf16[1,128,1024]{2,1,0:T(8,128)(2,1)S(1)}, u32[]{:S(2)}, u32[]{:S(2)}) collective-permute-start(bf16[1,128,1024]{2,1,0:T(8,128)(2,1)S(1)} %add_convert_fusion.13), channel_id=1, source_target_pairs={{0,16},{2,18},{4,20},{6,22},{8,24},{10,26},{12,28},{14,30},{16,0},... | collective-permute-start | bytes 786440 | tf_op jit(solution)/shard_map/ppermute | solution.py:12
  514.3 1.4 collective-permute-start.29
  (33 other events, 123.1 us)
where the time goes:
time: 524 us; the launch traced here: 518 us
  waiting for transfers between devices  232 us (44%)
  matrix products  122 us (23%)
  other arithmetic  46 us (9%)
  blocking collectives  40.1 us (8%)
  local copies, waits for them, and re-layouts  38.7 us (7%)
  starting transfers between devices  36 us (7%)
    ppermute x34, waiting for transfers between devices, over_seq(): return lax.ppermute(block, 'seq', route)  144 us
    ppermute x8, waiting for transfers between devices, swap_pair(): return lax.ppermute(block, 'wshard', [(0, 1), (1, 0)])  88.6 us
    dot_general x9, matrix products, mm_nt(): lax.dot_general(left, right, (((1,), (1,)), ((), ())), preferred_element_...  50.2 us
    psum x1, blocking collectives, local(): lax.psum(jnp.concatenate([spread, grad_gain_mix[None], grad_gain_ffn[None...  40.1 us
    dot_general x9, matrix products, mm(): return jnp.dot(left, right, preferred_element_type=F32)  39.3 us
    dot_general x5, matrix products, mm_tn(): lax.dot_general(left, right, (((0,), (0,)), ((), ())), preferred_element_...  32.9 us
    ppermute x34, starting transfers between devices, over_seq(): return lax.ppermute(block, 'seq', route)  26.3 us
    unnamed x125, local copies, waits for them, and re-layouts  18.5 us
  transfers between devices with their start and end apart: 42, of which 15 were waited for; matrix products, arithmetic and copies ran while one was open for 33% of the time, Pallas kernels for 0%

commit v1 on v0

--- a/solution.py
+++ b/solution.py
@@ -344,9 +344,12 @@
     spread = lax.dynamic_update_slice_in_dim(
         spread, grad_taps[:, features:], (1 - pair) * half_width + core * features, 1
     )
-    sums = lax.psum(
-        jnp.concatenate([spread, grad_gain_mix[None], grad_gain_ffn[None]], axis=0),
-        ("seq", "wshard"),
+    sums = jnp.sum(
+        lax.all_gather(
+            jnp.concatenate([spread, grad_gain_mix[None], grad_gain_ffn[None]], axis=0),
+            ("seq", "wshard"),
+        ),
+        axis=0,
     )
     sums = lax.dynamic_slice_in_dim(sums, pair * half_width, half_width, 1)
     return (

time: 524 us -> 555 us (1.059)
  blocking collectives: 40.1 us -> 72.7 us
    all_gather x0 -> x1, blocking collectives: none -> 72.7 us  [local(): lax.all_gather(jnp.concatenate([spread, grad_gain_mix[None], grad_gain_ff...]
    psum x1 -> x0, blocking collectives: 40.1 us -> none  [local(): lax.psum(jnp.concatenate([spread, grad_gain_mix[None], grad_gain_ffn[None...]
  transfers between devices with their start and end apart: 42 -> 42, of which waited for: 15 -> 15; matrix products, arithmetic and copies ran while one was open for 33% -> 34% of each run, Pallas kernels for 0% -> 0%
where the time goes in v1:
time: 555 us; the launch traced here: 548 us
  waiting for transfers between devices  230 us (41%)
  matrix products  122 us (22%)
  blocking collectives  72.7 us (13%)
  other arithmetic  46.1 us (8%)
  local copies, waits for them, and re-layouts  38.7 us (7%)
  starting transfers between devices  36.1 us (7%)
    ppermute x34, waiting for transfers between devices, over_seq(): return lax.ppermute(block, 'seq', route)  144 us
    ppermute x8, waiting for transfers between devices, swap_pair(): return lax.ppermute(block, 'wshard', [(0, 1), (1, 0)])  85.6 us
    all_gather x1, blocking collectives, local(): lax.all_gather(jnp.concatenate([spread, grad_gain_mix[None], grad_gain_ff...  72.7 us
    dot_general x9, matrix products, mm_nt(): lax.dot_general(left, right, (((1,), (1,)), ((), ())), preferred_element_...  50.2 us
    dot_general x9, matrix products, mm(): return jnp.dot(left, right, preferred_element_type=F32)  39.3 us
    dot_general x5, matrix products, mm_tn(): lax.dot_general(left, right, (((0,), (0,)), ((), ())), preferred_element_...  32.9 us
    ppermute x34, starting transfers between devices, over_seq(): return lax.ppermute(block, 'seq', route)  26.4 us
    unnamed x125, local copies, waits for them, and re-layouts  18.5 us
  transfers between devices with their start and end apart: 42, of which 15 were waited for; matrix products, arithmetic and copies ran while one was open for 34% of the time, Pallas kernels for 0%

profile of v1, /device:TPU:0, one launch (start us, length us, event | category | flops | bytes accessed | tf_op | source)
XLA Modules:
  0.0 548.3 jit_solution(3735923072541297260)
XLA Ops:
  0.7 3.2 copy.56
  9.0 3.0 collective-permute-start.2
  12.7 4.7 collective-permute-start.7
  17.4 1.9 fusion.80
  19.3 1.9 constant_dynamic-slice_fusion.25
  21.6 25.2 %collective-permute-done.1 = bf16[5,512]{1,0:T(8,128)(2,1)S(1)} collective-permute-done((bf16[5,512]{1,0:T(8,128)(2,1)S(1)}, bf16[5,512]{1,0:T(8,128)(2,1)S(1)}, u32[]{:S(2)}, u32[]{:S(2)}) %collective-permute-start.1) | collective-permute-done | bytes 5152 | tf_op jit(solution)/shard_map/ppermute | solution.py:24
  51.0 1.9 fusion.79
  52.9 2.0 fusion.78
  54.8 2.0 fusion.77
  56.8 1.9 fusion.76
  58.7 1.9 fusion.75
  60.6 2.4 fusion.86
  63.7 5.4 fusion.73
  73.1 4.2 convolution_convert_fusion.4
  77.5 1.5 collective-permute-start.17
  79.7 23.4 %collective-permute-done.17 = bf16[512,1024]{1,0:T(8,128)(2,1)} collective-permute-done((bf16[512,1024]{1,0:T(8,128)(2,1)}, bf16[512,1024]{1,0:T(8,128)(2,1)}, u32[]{:S(2)}, u32[]{:S(2)}) %collective-permute-start.17) | collective-permute-done | bytes 1048608 | tf_op jit(solution)/shard_map/ppermute | solution.py:24
  103.1 3.6 fusion.121
  106.8 1.9 fusion.125
  108.7 2.7 multiply_reduce_fusion
  111.9 1.6 collective-permute-start.11
  113.5 4.5 fusion.61
  118.0 4.5 fusion.69
  122.6 9.7 %multiply_convert_fusion.2 = (bf16[1024,1152]{1,0:T(8,128)(2,1)S(1)}, bf16[1024,1152]{1,0:T(8,128)(2,1)}, bf16[1024,1152]{1,0:T(8,128)(2,1)}) fusion(f32[1024,1152]{1,0:T(8,128)} %fusion.69, f32[1024,1152]{1,0:T(8,128)} %fusion.61, bf16[2304,1024]{1,0:T(8,128)(2,1)S(1)} %bitcast.222, s32[]{:T(128)S(6)} %select_n.227, ...), kind=kOutput, calls=%fused_computation.14 | convolution fusion | flops 2437808128 | bytes 20971524 | tf_op jit(solution)/shard_map/dot_general | solution.py:40
  132.3 6.1 %fusion.65 = f32[1024,1024]{1,0:T(8,128)S(1)} fusion(bf16[1024,1152]{1,0:T(8,128)(2,1)} %get-tuple-element.24, bf16[1024,2304]{1,0:T(8,128)(2,1)} %param.16, s32[]{:T(128)S(6)} %select_n.227), kind=kOutput, calls=%fused_computation.113 | convolution fusion | flops 2415919104 | bytes 8912900 | tf_op jit(solution)/shard_map/dot_general | solution.py:40
  138.8 5.0 add_convert_fusion.1
  145.1 3.3 convolution_convert_fusion.2
  149.6 4.5 fusion.59
  154.1 4.5 fusion.67
  158.6 11.4 %multiply_convert_fusion = (bf16[1024,1152]{1,0:T(8,128)(2,1)S(1)}, bf16[1024,1152]{1,0:T(8,128)(2,1)}, bf16[1024,1152]{1,0:T(8,128)(2,1)}) fusion(f32[1024,1152]{1,0:T(8,128)} %fusion.67, f32[1024,1152]{1,0:T(8,128)} %fusion.59, bf16[2304,1024]{1,0:T(8,128)(2,1)} %param.18, s32[]{:T(128)S(6)} %select_n.227, bf16[512,1024]{1,0:T(8,128)(2,1)} %collective-permute-done.18, ...), kind=kOutput, calls=%fused_computation.12 | convolution fusion | flops 2437808128 | bytes 20971524 | tf_op jit(solution)/shard_map/dot_general | solution.py:40
  170.1 6.1 %convolution_convert_fusion.1 = bf16[1024,1024]{1,0:T(8,128)(2,1)S(1)} fusion(bf16[1024,1152]{1,0:T(8,128)(2,1)} %get-tuple-element.28, bf16[2304,1024]{1,0:T(8,128)(2,1)} %param.18, s32[]{:T(128)S(6)} %select_n.227), kind=kOutput, calls=%fused_computation.96 | convolution fusion | flops 2416967680 | bytes 6815748 | tf_op jit(solution)/shard_map/dot_general | solution.py:32
  177.6 4.6 fusion.63
  182.2 3.6 add_convert_fusion
  187.7 9.3 %fusion.21 = bf16[1024,1152]{1,0:T(8,128)(2,1)S(1)} fusion(bf16[1024,1152]{1,0:T(8,128)(2,1)} %get-tuple-element.28, bf16[1024,1152]{1,0:T(8,128)(2,1)} %get-tuple-element.25, bf16[512,1024]{1,0:T(8,128)(2,1)} %collective-permute-done.18, bf16[512,1024]{1,0:T(8,128)(2,1)} %collective-permute-done.17, bf16[512,1024]{1,0:T(8,128)(2,1)} %collective-permute-done.15, ...), kind=kOutput, calls=%fused_computation.37 | convolution fusion | flops 4859232256 | bytes 11272192 | tf_op jit(solution)/shard_map/dot_general | solution.py:36
  198.4 1.5 collective-permute-start.38
  199.9 8.2 %fusion.26 = bf16[1024,1152]{1,0:T(8,128)(2,1)S(1)} fusion(bf16[1024,1152]{1,0:T(8,128)(2,1)} %copy-done.38, bf16[1024,1152]{1,0:T(8,128)(2,1)} %copy-done.37, bf16[512,1024]{1,0:T(8,128)(2,1)S(1)} %collective-permute-done.12, bf16[512,1024]{1,0:T(8,128)(2,1)S(1)} %collective-permute-done.11, bf16[1024,1024]{1,0:T(8,128)(2,1)S(1)} %multiply_convert_fusion.6), kind=kOutput, calls=%fused_computation.38 | convolution fusion | flops 4855037952 | bytes 11272192 | tf_op jit(solution)/shard_map/dot_general | solution.py:36
  210.2 8.8 %fusion.29 = bf16[1024,1152]{1,0:T(8,128)(2,1)S(1)} fusion(bf16[1024,1152]{1,0:T(8,128)(2,1)} %get-tuple-element.27, bf16[1024,1152]{1,0:T(8,128)(2,1)} %get-tuple-element.24, bf16[512,1024]{1,0:T(8,128)(2,1)} %copy-done.24, bf16[512,1024]{1,0:T(8,128)(2,1)} %copy-done.23, bf16[1024,1024]{1,0:T(8,128)(2,1)S(1)} %multiply_convert_fusion.6), kind=kOutput, calls=%fused_computation.39 | convolution fusion | flops 4855037952 | bytes 11272192 | tf_op jit(solution)/shard_map/dot_general | solution.py:36
  220.9 1.6 add_convert_fusion.5
  222.5 1.5 collective-permute-start.30
  224.1 1.6 add_convert_fusion.3
  225.7 1.8 collective-permute-done.38
  229.3 23.5 %collective-permute-done.34 = bf16[4,128,1152]{2,1,0:T(8,128)(2,1)} collective-permute-done((bf16[4,128,1152]{2,1,0:T(8,128)(2,1)}, bf16[4,128,1152]{2,1,0:T(8,128)(2,1)}, u32[]{:S(2)}, u32[]{:S(2)}) %collective-permute-start.34) | collective-permute-done | bytes 1179680 | tf_op jit(solution)/shard_map/ppermute | solution.py:12
  252.8 1.6 collective-permute-start.39
  255.6 21.7 %collective-permute-done.30 = bf16[4,128,1152]{2,1,0:T(8,128)(2,1)S(1)} collective-permute-done((bf16[4,128,1152]{2,1,0:T(8,128)(2,1)S(1)}, bf16[4,128,1152]{2,1,0:T(8,128)(2,1)S(1)}, u32[]{:S(2)}, u32[]{:S(2)}) %collective-permute-start.30) | collective-permute-done | bytes 1179680 | tf_op jit(solution)/shard_map/ppermute | solution.py:12
  277.3 1.6 collective-permute-start.35
  280.6 12.9 %collective-permute-done.35 = bf16[2,128,1152]{2,1,0:T(8,128)(2,1)S(1)} collective-permute-done((bf16[2,128,1152]{2,1,0:T(8,128)(2,1)S(1)}, bf16[2,128,1152]{2,1,0:T(8,128)(2,1)S(1)}, u32[]{:S(2)}, u32[]{:S(2)}) %collective-permute-start.35) | collective-permute-done | bytes 589856 | tf_op jit(solution)/shard_map/ppermute | solution.py:12
  295.3 9.3 %collective-permute-done.31 = bf16[2,128,1152]{2,1,0:T(8,128)(2,1)S(1)} collective-permute-done((bf16[2,128,1152]{2,1,0:T(8,128)(2,1)S(1)}, bf16[2,128,1152]{2,1,0:T(8,128)(2,1)S(1)}, u32[]{:S(2)}, u32[]{:S(2)}) %collective-permute-start.31) | collective-permute-done | bytes 589856 | tf_op jit(solution)/shard_map/ppermute | solution.py:12
  304.6 2.6 collective-permute-start.40
  307.3 11.9 %collective-permute-done.40 = bf16[1,128,1152]{2,1,0:T(8,128)(2,1)S(1)} collective-permute-done((bf16[1,128,1152]{2,1,0:T(8,128)(2,1)S(1)}, bf16[1,128,1152]{2,1,0:T(8,128)(2,1)S(1)}, u32[]{:S(2)}, u32[]{:S(2)}) %collective-permute-start.40) | collective-permute-done | bytes 294944 | tf_op jit(solution)/shard_map/ppermute | solution.py:12
  320.3 14.0 %collective-permute-done.36 = bf16[1,128,1152]{2,1,0:T(8,128)(2,1)S(1)} collective-permute-done((bf16[1,128,1152]{2,1,0:T(8,128)(2,1)S(1)}, bf16[1,128,1152]{2,1,0:T(8,128)(2,1)S(1)}, u32[]{:S(2)}, u32[]{:S(2)}) %collective-permute-start.36) | collective-permute-done | bytes 294944 | tf_op jit(solution)/shard_map/ppermute | solution.py:12
  336.8 11.6 %collective-permute-done.32 = bf16[1,128,1152]{2,1,0:T(8,128)(2,1)S(1)} collective-permute-done((bf16[1,128,1152]{2,1,0:T(8,128)(2,1)S(1)}, bf16[1,128,1152]{2,1,0:T(8,128)(2,1)S(1)}, u32[]{:S(2)}, u32[]{:S(2)}) %collective-permute-start.32) | collective-permute-done | bytes 294944 | tf_op jit(solution)/shard_map/ppermute | solution.py:12
  349.6 4.0 fusion.122
  359.0 2.5 collective-permute-done.22
  361.6 1.6 convolution_multiply_fusion
  364.3 4.6 multiply_reduce_fusion.6
  372.1 2.9 convolution_convert_fusion.5
  375.1 3.7 convolution_convert_fusion
  384.8 3.7 convolution_convert_fusion.3
  391.0 37.0 %collective-permute-done.25 = bf16[8,128,1024]{2,1,0:T(8,128)(2,1)S(1)} collective-permute-done((bf16[8,128,1024]{2,1,0:T(8,128)(2,1)S(1)}, bf16[8,128,1024]{2,1,0:T(8,128)(2,1)S(1)}, u32[]{:S(2)}, u32[]{:S(2)}) %collective-permute-start.25) | collective-permute-done | bytes 2097184 | tf_op jit(solution)/shard_map/ppermute | solution.py:24
  428.4 3.0 collective-permute-start.26
  432.3 22.5 %collective-permute-done.26 = bf16[4,128,1024]{2,1,0:T(8,128)(2,1)S(1)} collective-permute-done((bf16[4,128,1024]{2,1,0:T(8,128)(2,1)S(1)}, bf16[4,128,1024]{2,1,0:T(8,128)(2,1)S(1)}, u32[]{:S(2)}, u32[]{:S(2)}) %collective-permute-start.26) | collective-permute-done | bytes 1048608 | tf_op jit(solution)/shard_map/ppermute | solution.py:12
  455.3 2.0 multiply_add_fusion
  457.3 11.3 %collective-permute-done.27 = bf16[2,128,1024]{2,1,0:T(8,128)(2,1)S(1)} collective-permute-done((bf16[2,128,1024]{2,1,0:T(8,128)(2,1)S(1)}, bf16[2,128,1024]{2,1,0:T(8,128)(2,1)S(1)}, u32[]{:S(2)}, u32[]{:S(2)}) %collective-permute-start.27) | collective-permute-done | bytes 524320 | tf_op jit(solution)/shard_map/ppermute | solution.py:12
  469.4 72.7 %all-gather.1 = f32[32,5,1024]{2,1,0:T(8,128)S(1)} all-gather(f32[1,5,1024]{2,1,0:T(8,128)S(1)} %maximum_bitcast_fusion), channel_id=2, replica_groups=mesh['seq'=16,'wshard'=2] {'seq','wshard'}, dimensions={0}, use_global_device_ids=true | all-gather | bytes 675840 | tf_op jit(solution)/shard_map/all_gather | solution.py:348
  543.5 1.5 convert_add_fusion.5
  (311 shorter events, 64.2 us)
Async XLA Ops:
  3.8 8.8 %copy-start.34 = (s32[4,128]{1,0:T(4,128)S(1)}, s32[4,128]{1,0:T(4,128)}, u32[]{:S(2)}) copy-start(s32[4,128]{1,0:T(4,128)} %param.12) | copy-start | bytes 6148
  5.7 13.6 %copy-start.35 = (bf16[512]{0:T(512)(128)(2,1)S(1)}, bf16[512]{0:T(512)(128)(2,1)}, u32[]{:S(2)}) copy-start(bf16[512]{0:T(512)(128)(2,1)} %param.20) | copy-start | bytes 3076
  5.7 13.6 %copy-start.36 = (bf16[512]{0:T(512)(128)(2,1)S(1)}, bf16[512]{0:T(512)(128)(2,1)}, u32[]{:S(2)}) copy-start(bf16[512]{0:T(512)(128)(2,1)} %param.21) | copy-start | bytes 3076
  5.7 41.8 %collective-permute-start.5 = (bf16[4,2,1152]{2,0,1:T(4,128)(2,1)S(1)}, bf16[4,2,1152]{2,0,1:T(4,128)(2,1)S(1)}, u32[]{:S(2)}, u32[]{:S(2)}) collective-permute-start(bf16[4,2,1152]{2,0,1:T(4,128)(2,1)S(1)} %get-tuple-element.69), channel_id=1, source_target_pairs={{4,0},{8,4},{12,8},{16,12},{20,16},{24,20},{28,24},{5,1},{9,5},{13... | collective-permute-start | bytes 55304 | tf_op jit(solution)/shard_map/ppermute | solution.py:12
  7.0 41.0 %collective-permute-start.6 = (bf16[4,2,1152]{2,0,1:T(4,128)(2,1)S(1)}, bf16[4,2,1152]{2,0,1:T(4,128)(2,1)S(1)}, u32[]{:S(2)}, u32[]{:S(2)}) collective-permute-start(bf16[4,2,1152]{2,0,1:T(4,128)(2,1)S(1)} %get-tuple-element.69), channel_id=1, source_target_pairs={{4,2},{8,6},{12,10},{16,14},{20,18},{24,22},{28,26},{5,3},{9,7},{1... | collective-permute-start | bytes 55304 | tf_op jit(solution)/shard_map/ppermute | solution.py:12
  7.7 13.5 %copy-start.33 = (bf16[3,512]{1,0:T(4,128)(2,1)S(1)}, bf16[3,512]{1,0:T(4,128)(2,1)}, u32[]{:S(2)}) copy-start(bf16[3,512]{1,0:T(4,128)(2,1)} %param.19) | copy-start | bytes 9220
  9.0 38.6 %copy-start.6 = (bf16[4,128,1024]{2,1,0:T(8,128)(2,1)S(1)}, bf16[4,128,1024]{2,1,0:T(8,128)(2,1)}, u32[]{:S(2)}) copy-start(bf16[4,128,1024]{2,1,0:T(8,128)(2,1)} %param.11) | copy-start | bytes 3145732
  9.0 42.0 %collective-permute-start.2 = (bf16[3,1024,256]{2,1,0:T(8,128)(2,1)}, bf16[3,1024,256]{2,1,0:T(8,128)(2,1)}, u32[]{:S(2)}, u32[]{:S(2)}) collective-permute-start(bf16[3,1024,256]{2,1,0:T(8,128)(2,1)} %dynamic-slice_bitcast_fusion), channel_id=1, source_target_pairs={{0,1},{1,0},{2,3},{3,2},{4,5},{5,4},{6,7},{7,6},{8,9},{9,8},{10,11... | collective-permute-start | bytes 4718600 | tf_op jit(solution)/shard_map/ppermute | solution.py:24
  11.9 37.5 %collective-permute-start.3 = (bf16[4,2,1152]{2,0,1:T(4,128)(2,1)S(1)}, bf16[4,2,1152]{2,0,1:T(4,128)(2,1)S(1)}, u32[]{:S(2)}, u32[]{:S(2)}) collective-permute-start(bf16[4,2,1152]{2,0,1:T(4,128)(2,1)S(1)} %get-tuple-element.68), channel_id=1, source_target_pairs={{2,4},{6,8},{10,12},{14,16},{18,20},{22,24},{26,28},{3,5},{7,9},{1... | collective-permute-start | bytes 55304 | tf_op jit(solution)/shard_map/ppermute | solution.py:12
  12.7 8.6 %collective-permute-start.7 = (s32[4,128]{0,1:T(8,128)S(1)}, s32[4,128]{0,1:T(8,128)S(1)}, u32[]{:S(2)}, u32[]{:S(2)}) collective-permute-start(s32[4,128]{0,1:T(8,128)S(1)} %copy.57), channel_id=1, source_target_pairs={{0,2},{2,0},{4,6},{6,4},{8,10},{10,8},{12,14},{14,12},{16,18},{18,... | collective-permute-start | bytes 6152 | tf_op jit(solution)/shard_map/ppermute | solution.py:12
  21.3 25.4 %collective-permute-start.1 = (bf16[5,512]{1,0:T(8,128)(2,1)S(1)}, bf16[5,512]{1,0:T(8,128)(2,1)S(1)}, u32[]{:S(2)}, u32[]{:S(2)}) collective-permute-start(bf16[5,512]{1,0:T(8,128)(2,1)S(1)} %pad_maximum_fusion.25), channel_id=1, source_target_pairs={{0,1},{1,0},{2,3},{3,2},{4,5},{5,4},{6,7},{7,6},{8,9},{9,8},{10,11... | collective-permute-start | bytes 15368 | tf_op jit(solution)/shard_map/ppermute | solution.py:24
  46.7 2.7 collective-permute-start.4
  47.4 15.7 %copy-start.28 = (f32[1,1024]{1,0:T(1,128)}, f32[1,1024]{1,0:T(1,128)S(1)}, u32[]{:S(2)}) copy-start(f32[1,1024]{1,0:T(1,128)S(1)} %get-tuple-element.90) | copy-start | bytes 12292
  47.5 2.9 collective-permute-start
  48.0 25.1 %collective-permute-start.8 = (bf16[256,1024]{1,0:T(8,128)(2,1)}, bf16[256,1024]{1,0:T(8,128)(2,1)}, u32[]{:S(2)}, u32[]{:S(2)}) collective-permute-start(bf16[256,1024]{1,0:T(8,128)(2,1)} %constant_dynamic-slice_fusion.25), channel_id=1, source_target_pairs={{0,1},{1,0},{2,3},{3,2},{4,5},{5,4},{6,7},{7,6},{8,9},{9,8},{10,11... | collective-permute-start | bytes 1572872 | tf_op jit(solution)/shard_map/ppermute | solution.py:24
  50.4 12.7 %copy-start.7 = (bf16[512,1024]{1,0:T(8,128)(2,1)}, bf16[512,1024]{1,0:T(8,128)(2,1)S(1)}, u32[]{:S(2)}) copy-start(bf16[512,1024]{1,0:T(8,128)(2,1)S(1)} %collective-permute-done) | copy-start | bytes 3145732
  50.9 28.2 %copy-start.31 = (f32[1024]{0:T(1024)}, f32[1024]{0:T(1024)S(1)}, u32[]{:S(2)}) copy-start(f32[1024]{0:T(1024)S(1)} %add_rsqrt_fusion.1) | copy-start | bytes 12292
  77.2 29.5 %collective-permute-start.9 = (bf16[1024,1024]{1,0:T(8,128)(2,1)}, bf16[1024,1024]{1,0:T(8,128)(2,1)}, u32[]{:S(2)}, u32[]{:S(2)}) collective-permute-start(bf16[1024,1024]{1,0:T(8,128)(2,1)} %convolution_convert_fusion.4), channel_id=1, source_target_pairs={{0,2},{2,0},{4,6},{6,4},{8,10},{10,8},{12,14},{14,12},{16,18},{18,... | collective-permute-start | bytes 6291464 | tf_op jit(solution)/shard_map/ppermute | solution.py:12
  77.5 25.7 %collective-permute-start.17 = (bf16[512,1024]{1,0:T(8,128)(2,1)}, bf16[512,1024]{1,0:T(8,128)(2,1)}, u32[]{:S(2)}, u32[]{:S(2)}) collective-permute-start(bf16[512,1024]{1,0:T(8,128)(2,1)} %bitcast.18), channel_id=1, source_target_pairs={{0,1},{1,0},{2,3},{3,2},{4,5},{5,4},{6,7},{7,6},{8,9},{9,8},{10,11... | collective-permute-start | bytes 3145736 | tf_op jit(solution)/shard_map/ppermute | solution.py:24
  78.9 43.6 %collective-permute-start.15 = (bf16[512,1024]{1,0:T(8,128)(2,1)}, bf16[512,1024]{1,0:T(8,128)(2,1)}, u32[]{:S(2)}, u32[]{:S(2)}) collective-permute-start(bf16[512,1024]{1,0:T(8,128)(2,1)} %bitcast.18), channel_id=1, source_target_pairs={{0,2},{2,0},{4,6},{6,4},{8,10},{10,8},{12,14},{14,12},{16,18},{18,... | collective-permute-start | bytes 3145736 | tf_op jit(solution)/shard_map/ppermute | solution.py:12
  103.1 55.5 %collective-permute-start.18 = (bf16[512,1024]{1,0:T(8,128)(2,1)}, bf16[512,1024]{1,0:T(8,128)(2,1)}, u32[]{:S(2)}, u32[]{:S(2)}) collective-permute-start(bf16[512,1024]{1,0:T(8,128)(2,1)} %collective-permute-done.17), channel_id=1, source_target_pairs={{0,2},{2,0},{4,6},{6,4},{8,10},{10,8},{12,14},{14,12},{16,18},{18,... | collective-permute-start | bytes 3145736 | tf_op jit(solution)/shard_map/ppermute | solution.py:12
  111.9 26.5 %collective-permute-start.11 = (bf16[512,1024]{1,0:T(8,128)(2,1)S(1)}, bf16[512,1024]{1,0:T(8,128)(2,1)S(1)}, u32[]{:S(2)}, u32[]{:S(2)}) collective-permute-start(bf16[512,1024]{1,0:T(8,128)(2,1)S(1)} %slice.503), channel_id=1, source_target_pairs={{0,1},{1,0},{2,3},{3,2},{4,5},{5,4},{6,7},{7,6},{8,9},{9,8},{10,11... | collective-permute-start | bytes 3145736 | tf_op jit(solution)/shard_map/ppermute | solution.py:24
  113.5 9.0 %slice-start.2 = ((s8[4718592]{0:T(1024)(128)(4,1)}), s8[4194304]{0:T(1024)(128)(4,1)S(1)}, s32[]{:S(2)}) async-start(s8[4718592]{0:T(1024)(128)(4,1)} %bitcast.221), calls=%async_computation.2 | async-start | bytes 8388608
  138.4 61.4 %copy-start.23 = (bf16[512,1024]{1,0:T(8,128)(2,1)}, bf16[512,1024]{1,0:T(8,128)(2,1)S(1)}, u32[]{:S(2)}) copy-start(bf16[512,1024]{1,0:T(8,128)(2,1)S(1)} %collective-permute-done.11) | copy-start | bytes 3145732
  138.4 11.1 %collective-permute-start.12 = (bf16[512,1024]{1,0:T(8,128)(2,1)S(1)}, bf16[512,1024]{1,0:T(8,128)(2,1)S(1)}, u32[]{:S(2)}, u32[]{:S(2)}) collective-permute-start(bf16[512,1024]{1,0:T(8,128)(2,1)S(1)} %collective-permute-done.11), channel_id=1, source_target_pairs={{0,2},{2,0},{4,6},{6,4},{8,10},{10,8},{12,14},{14,12},{16,18},{18,... | collective-permute-start | bytes 3145736 | tf_op jit(solution)/shard_map/ppermute | solution.py:12
  138.8 10.9 %slice-start.10 = ((s8[4718592]{0:T(1024)(128)(4,1)}), s8[524288]{0:T(1024)(128)(4,1)S(1)}, s32[]{:S(2)}) async-start(s8[4718592]{0:T(1024)(128)(4,1)} %bitcast.229), calls=%async_computation.10 | async-start | bytes 1048576
  144.8 203.8 %collective-permute-start.16 = (bf16[512,1024]{1,0:T(8,128)(2,1)}, bf16[512,1024]{1,0:T(8,128)(2,1)S(1)}, u32[]{:S(2)}, u32[]{:S(2)}) collective-permute-start(bf16[512,1024]{1,0:T(8,128)(2,1)} %slice.507), channel_id=1, source_target_pairs={{0,2},{2,0},{4,6},{6,4},{8,10},{10,8},{12,14},{14,12},{16,18},{18,... | collective-permute-start | bytes 3145736 | tf_op jit(solution)/shard_map/ppermute | solution.py:12
  149.5 50.4 %copy-start.24 = (bf16[512,1024]{1,0:T(8,128)(2,1)}, bf16[512,1024]{1,0:T(8,128)(2,1)S(1)}, u32[]{:S(2)}) copy-start(bf16[512,1024]{1,0:T(8,128)(2,1)S(1)} %collective-permute-done.12) | copy-start | bytes 3145732
  170.1 12.0 %copy-start.38 = (bf16[1024,1152]{1,0:T(8,128)(2,1)}, bf16[1024,1152]{1,0:T(8,128)(2,1)S(1)}, u32[]{:S(2)}) copy-start(bf16[1024,1152]{1,0:T(8,128)(2,1)S(1)} %get-tuple-element.26) | copy-start | bytes 7077892
  170.1 7.5 %copy-start.39 = (bf16[1024,1152]{1,0:T(8,128)(2,1)S(1)}, bf16[1024,1152]{1,0:T(8,128)(2,1)}, u32[]{:S(2)}) copy-start(bf16[1024,1152]{1,0:T(8,128)(2,1)} %get-tuple-element.27) | copy-start | bytes 7077892
  170.1 12.1 %slice-start.12 = ((s8[4718592]{0:T(1024)(128)(4,1)}), s8[4194304]{0:T(1024)(128)(4,1)S(1)}, s32[]{:S(2)}) async-start(s8[4718592]{0:T(1024)(128)(4,1)} %bitcast.231), calls=%async_computation.12 | async-start | bytes 8388608
  177.3 42.1 %collective-permute-start.13 = (bf16[512,1024]{1,0:T(8,128)(2,1)}, bf16[512,1024]{1,0:T(8,128)(2,1)}, u32[]{:S(2)}, u32[]{:S(2)}) collective-permute-start(bf16[512,1024]{1,0:T(8,128)(2,1)} %slice.505), channel_id=1, source_target_pairs={{0,2},{2,0},{4,6},{6,4},{8,10},{10,8},{12,14},{14,12},{16,18},{18,... | collective-permute-start | bytes 3145736 | tf_op jit(solution)/shard_map/ppermute | solution.py:12
  187.4 35.1 %collective-permute-start.19 = (bf16[512,1024]{1,0:T(8,128)(2,1)}, bf16[512,1024]{1,0:T(8,128)(2,1)}, u32[]{:S(2)}, u32[]{:S(2)}) collective-permute-start(bf16[512,1024]{1,0:T(8,128)(2,1)} %slice.509), channel_id=1, source_target_pairs={{0,2},{2,0},{4,6},{6,4},{8,10},{10,8},{12,14},{14,12},{16,18},{18,... | collective-permute-start | bytes 3145736 | tf_op jit(solution)/shard_map/ppermute | solution.py:12
  198.4 29.1 %collective-permute-start.38 = (bf16[4,128,1152]{2,1,0:T(8,128)(2,1)}, bf16[4,128,1152]{2,1,0:T(8,128)(2,1)}, u32[]{:S(2)}, u32[]{:S(2)}) collective-permute-start(bf16[4,128,1152]{2,1,0:T(8,128)(2,1)} %pad_maximum_fusion.16), channel_id=1, source_target_pairs={{0,4},{2,6},{4,0},{6,2},{8,12},{10,14},{12,8},{14,10},{16,20},{18,... | collective-permute-start | bytes 3538952 | tf_op jit(solution)/shard_map/ppermute | solution.py:12
  209.7 43.1 %collective-permute-start.34 = (bf16[4,128,1152]{2,1,0:T(8,128)(2,1)}, bf16[4,128,1152]{2,1,0:T(8,128)(2,1)}, u32[]{:S(2)}, u32[]{:S(2)}) collective-permute-start(bf16[4,128,1152]{2,1,0:T(8,128)(2,1)} %pad_maximum_fusion.15), channel_id=1, source_target_pairs={{0,4},{2,6},{4,0},{6,2},{8,12},{10,14},{12,8},{14,10},{16,20},{18,... | collective-permute-start | bytes 3538952 | tf_op jit(solution)/shard_map/ppermute | solution.py:12
  220.2 129.4 %collective-permute-start.10 = (bf16[512,1024]{1,0:T(8,128)(2,1)S(1)}, bf16[512,1024]{1,0:T(8,128)(2,1)S(1)}, u32[]{:S(2)}, u32[]{:S(2)}) collective-permute-start(bf16[512,1024]{1,0:T(8,128)(2,1)S(1)} %copy-done.22), channel_id=1, source_target_pairs={{0,2},{2,0},{4,6},{6,4},{8,10},{10,8},{12,14},{14,12},{16,18},{18,... | collective-permute-start | bytes 3145736 | tf_op jit(solution)/shard_map/ppermute | solution.py:12
  222.5 54.8 %collective-permute-start.30 = (bf16[4,128,1152]{2,1,0:T(8,128)(2,1)S(1)}, bf16[4,128,1152]{2,1,0:T(8,128)(2,1)S(1)}, u32[]{:S(2)}, u32[]{:S(2)}) collective-permute-start(bf16[4,128,1152]{2,1,0:T(8,128)(2,1)S(1)} %pad_maximum_fusion.14), channel_id=1, source_target_pairs={{0,4},{2,6},{4,0},{6,2},{8,12},{10,14},{12,8},{14,10},{16,20},{18,... | collective-permute-start | bytes 3538952 | tf_op jit(solution)/shard_map/ppermute | solution.py:12
  227.5 122.1 %collective-permute-start.14 = (bf16[512,1024]{1,0:T(8,128)(2,1)S(1)}, bf16[512,1024]{1,0:T(8,128)(2,1)S(1)}, u32[]{:S(2)}, u32[]{:S(2)}) collective-permute-start(bf16[512,1024]{1,0:T(8,128)(2,1)S(1)} %add_convert_fusion.5), channel_id=1, source_target_pairs={{0,1},{1,0},{2,3},{3,2},{4,5},{5,4},{6,7},{7,6},{8,9},{9,8},{10,11... | collective-permute-start | bytes 3145736 | tf_op jit(solution)/shard_map/ppermute | solution.py:24
  252.8 26.2 %collective-permute-start.39 = (bf16[2,128,1152]{2,1,0:T(8,128)(2,1)S(1)}, bf16[2,128,1152]{2,1,0:T(8,128)(2,1)S(1)}, u32[]{:S(2)}, u32[]{:S(2)}) collective-permute-start(bf16[2,128,1152]{2,1,0:T(8,128)(2,1)S(1)} %add_convert_fusion.6), channel_id=1, source_target_pairs={{0,8},{2,10},{4,12},{6,14},{8,0},{10,2},{12,4},{14,6},{16,24},{18,... | collective-permute-start | bytes 1769480 | tf_op jit(solution)/shard_map/ppermute | solution.py:12
  277.3 16.3 %collective-permute-start.35 = (bf16[2,128,1152]{2,1,0:T(8,128)(2,1)S(1)}, bf16[2,128,1152]{2,1,0:T(8,128)(2,1)S(1)}, u32[]{:S(2)}, u32[]{:S(2)}) collective-permute-start(bf16[2,128,1152]{2,1,0:T(8,128)(2,1)S(1)} %add_convert_fusion.7), channel_id=1, source_target_pairs={{0,8},{2,10},{4,12},{6,14},{8,0},{10,2},{12,4},{14,6},{16,24},{18,... | collective-permute-start | bytes 1769480 | tf_op jit(solution)/shard_map/ppermute | solution.py:12
  279.0 25.6 %collective-permute-start.31 = (bf16[2,128,1152]{2,1,0:T(8,128)(2,1)S(1)}, bf16[2,128,1152]{2,1,0:T(8,128)(2,1)S(1)}, u32[]{:S(2)}, u32[]{:S(2)}) collective-permute-start(bf16[2,128,1152]{2,1,0:T(8,128)(2,1)S(1)} %add_convert_fusion.8), channel_id=1, source_target_pairs={{0,8},{2,10},{4,12},{6,14},{8,0},{10,2},{12,4},{14,6},{16,24},{18,... | collective-permute-start | bytes 1769480 | tf_op jit(solution)/shard_map/ppermute | solution.py:12
  293.6 55.1 %collective-permute-start.20 = (bf16[512,1024]{1,0:T(8,128)(2,1)S(1)}, bf16[512,1024]{1,0:T(8,128)(2,1)S(1)}, u32[]{:S(2)}, u32[]{:S(2)}) collective-permute-start(bf16[512,1024]{1,0:T(8,128)(2,1)S(1)} %add_convert_fusion.3), channel_id=1, source_target_pairs={{0,1},{1,0},{2,3},{3,2},{4,5},{5,4},{6,7},{7,6},{8,9},{9,8},{10,11... | collective-permute-start | bytes 3145736 | tf_op jit(solution)/shard_map/ppermute | solution.py:24
  304.6 14.6 %collective-permute-start.40 = (bf16[1,128,1152]{2,1,0:T(8,128)(2,1)S(1)}, bf16[1,128,1152]{2,1,0:T(8,128)(2,1)S(1)}, u32[]{:S(2)}, u32[]{:S(2)}) collective-permute-start(bf16[1,128,1152]{2,1,0:T(8,128)(2,1)S(1)} %add_convert_fusion.10), channel_id=1, source_target_pairs={{0,16},{2,18},{4,20},{6,22},{8,24},{10,26},{12,28},{14,30},{16,0},... | collective-permute-start | bytes 884744 | tf_op jit(solution)/shard_map/ppermute | solution.py:12
  319.2 15.1 %collective-permute-start.36 = (bf16[1,128,1152]{2,1,0:T(8,128)(2,1)S(1)}, bf16[1,128,1152]{2,1,0:T(8,128)(2,1)S(1)}, u32[]{:S(2)}, u32[]{:S(2)}) collective-permute-start(bf16[1,128,1152]{2,1,0:T(8,128)(2,1)S(1)} %add_convert_fusion.11), channel_id=1, source_target_pairs={{0,16},{2,18},{4,20},{6,22},{8,24},{10,26},{12,28},{14,30},{16,0},... | collective-permute-start | bytes 884744 | tf_op jit(solution)/shard_map/ppermute | solution.py:12
  334.3 14.2 %collective-permute-start.32 = (bf16[1,128,1152]{2,1,0:T(8,128)(2,1)S(1)}, bf16[1,128,1152]{2,1,0:T(8,128)(2,1)S(1)}, u32[]{:S(2)}, u32[]{:S(2)}) collective-permute-start(bf16[1,128,1152]{2,1,0:T(8,128)(2,1)S(1)} %add_convert_fusion.12), channel_id=1, source_target_pairs={{0,16},{2,18},{4,20},{6,22},{8,24},{10,26},{12,28},{14,30},{16,0},... | collective-permute-start | bytes 884744 | tf_op jit(solution)/shard_map/ppermute | solution.py:12
  353.6 10.7 %collective-permute-start.21 = (bf16[512,1024]{1,0:T(8,128)(2,1)}, bf16[512,1024]{1,0:T(8,128)(2,1)}, u32[]{:S(2)}, u32[]{:S(2)}) collective-permute-start(bf16[512,1024]{1,0:T(8,128)(2,1)} %get-tuple-element.19), channel_id=1, source_target_pairs={{0,2},{2,0},{4,6},{6,4},{8,10},{10,8},{12,14},{14,12},{16,18},{18,... | collective-permute-start | bytes 3145736 | tf_op jit(solution)/shard_map/ppermute | solution.py:12
  355.9 5.7 %collective-permute-start.22 = (bf16[4,2,1024]{2,1,0:T(2,128)(2,1)S(1)}, bf16[4,2,1024]{2,1,0:T(2,128)(2,1)S(1)}, u32[]{:S(2)}, u32[]{:S(2)}) collective-permute-start(bf16[4,2,1024]{2,1,0:T(2,128)(2,1)S(1)} %slice.515), channel_id=1, source_target_pairs={{4,0},{8,4},{12,8},{16,12},{20,16},{24,20},{28,24},{5,1},{9,5},{13... | collective-permute-start | bytes 49160 | tf_op jit(solution)/shard_map/ppermute | solution.py:12
  357.2 4.4 collective-permute-start.23
  358.5 4.7 collective-permute-start.41
  359.0 22.1 %collective-permute-start.37 = (bf16[64,1152]{1,0:T(8,128)(2,1)}, bf16[64,1152]{1,0:T(8,128)(2,1)}, u32[]{:S(2)}, u32[]{:S(2)}) collective-permute-start(bf16[64,1152]{1,0:T(8,128)(2,1)} %fusion.82), channel_id=1, source_target_pairs={{0,2},{2,0},{4,6},{6,4},{8,10},{10,8},{12,14},{14,12},{16,18},{18,... | collective-permute-start | bytes 442376 | tf_op jit(solution)/shard_map/ppermute | solution.py:12
  361.6 20.6 %collective-permute-start.33 = (bf16[64,1152]{1,0:T(8,128)(2,1)}, bf16[64,1152]{1,0:T(8,128)(2,1)}, u32[]{:S(2)}, u32[]{:S(2)}) collective-permute-start(bf16[64,1152]{1,0:T(8,128)(2,1)} %fusion.81), channel_id=1, source_target_pairs={{0,2},{2,0},{4,6},{6,4},{8,10},{10,8},{12,14},{14,12},{16,18},{18,... | collective-permute-start | bytes 442376 | tf_op jit(solution)/shard_map/ppermute | solution.py:12
  363.2 7.6 %slice-start = ((s8[6291456]{0:T(1024)(128)(4,1)}), s8[4194304]{0:T(1024)(128)(4,1)S(1)}, s32[]{:S(2)}) async-start(s8[6291456]{0:T(1024)(128)(4,1)} %bitcast.141), calls=%async_computation | async-start | bytes 8388608
  379.6 48.4 %collective-permute-start.25 = (bf16[8,128,1024]{2,1,0:T(8,128)(2,1)S(1)}, bf16[8,128,1024]{2,1,0:T(8,128)(2,1)S(1)}, u32[]{:S(2)}, u32[]{:S(2)}) collective-permute-start(bf16[8,128,1024]{2,1,0:T(8,128)(2,1)S(1)} %dynamic-slice_dynamic-update-slice_fusion), channel_id=1, source_target_pairs={{0,1},{1,0},{2,3},{3,2},{4,5},{5,4},{6,7},{7,6},{8,9},{9,8},{10,11... | collective-permute-start | bytes 6291464 | tf_op jit(solution)/shard_map/ppermute | solution.py:24
  388.5 42.9 %collective-permute-start.24 = (bf16[512,1024]{1,0:T(8,128)(2,1)S(1)}, bf16[512,1024]{1,0:T(8,128)(2,1)S(1)}, u32[]{:S(2)}, u32[]{:S(2)}) collective-permute-start(bf16[512,1024]{1,0:T(8,128)(2,1)S(1)} %slice.522), channel_id=1, source_target_pairs={{0,2},{2,0},{4,6},{6,4},{8,10},{10,8},{12,14},{14,12},{16,18},{18,... | collective-permute-start | bytes 3145736 | tf_op jit(solution)/shard_map/ppermute | solution.py:12
  390.8 77.8 %copy-start.11 = (bf16[8,128,1024]{2,1,0:T(8,128)(2,1)}, bf16[8,128,1024]{2,1,0:T(8,128)(2,1)S(1)}, u32[]{:S(2)}) copy-start(bf16[8,128,1024]{2,1,0:T(8,128)(2,1)S(1)} %pad_maximum_fusion.6) | copy-start | bytes 6291460
  390.8 40.7 %copy-start.5 = (f32[1024,1024]{1,0:T(8,128)S(1)}, f32[1024,1024]{1,0:T(8,128)}, u32[]{:S(2)}) copy-start(f32[1024,1024]{1,0:T(8,128)} %fusion.121) | copy-start | bytes 12582916
  391.0 40.5 %copy-start.30 = (f32[512]{0:T(512)S(1)}, f32[512]{0:T(512)}, u32[]{:S(2)}) copy-start(f32[512]{0:T(512)} %slice.414) | copy-start | bytes 6148
  428.0 40.6 %copy-start.17 = (bf16[8,128,1024]{2,1,0:T(8,128)(2,1)}, bf16[8,128,1024]{2,1,0:T(8,128)(2,1)S(1)}, u32[]{:S(2)}) copy-start(bf16[8,128,1024]{2,1,0:T(8,128)(2,1)S(1)} %collective-permute-done.25) | copy-start | bytes 6291460
  428.4 26.4 %collective-permute-start.26 = (bf16[4,128,1024]{2,1,0:T(8,128)(2,1)S(1)}, bf16[4,128,1024]{2,1,0:T(8,128)(2,1)S(1)}, u32[]{:S(2)}, u32[]{:S(2)}) collective-permute-start(bf16[4,128,1024]{2,1,0:T(8,128)(2,1)S(1)} %add_convert_fusion.2), channel_id=1, source_target_pairs={{0,4},{2,6},{4,0},{6,2},{8,12},{10,14},{12,8},{14,10},{16,20},{18,... | collective-permute-start | bytes 3145736 | tf_op jit(solution)/shard_map/ppermute | solution.py:12
  431.4 23.9 %copy-start.10 = (f32[512,1024]{1,0:T(8,128)S(1)}, f32[512,1024]{1,0:T(8,128)}, u32[]{:S(2)}) copy-start(f32[512,1024]{1,0:T(8,128)} %get-tuple-element.20) | copy-start | bytes 6291460
  454.8 13.8 %copy-start.25 = (bf16[4,128,1024]{2,1,0:T(8,128)(2,1)}, bf16[4,128,1024]{2,1,0:T(8,128)(2,1)S(1)}, u32[]{:S(2)}) copy-start(bf16[4,128,1024]{2,1,0:T(8,128)(2,1)S(1)} %collective-permute-done.26) | copy-start | bytes 3145732
  455.1 13.5 %collective-permute-start.27 = (bf16[2,128,1024]{2,1,0:T(8,128)(2,1)S(1)}, bf16[2,128,1024]{2,1,0:T(8,128)(2,1)S(1)}, u32[]{:S(2)}, u32[]{:S(2)}) collective-permute-start(bf16[2,128,1024]{2,1,0:T(8,128)(2,1)S(1)} %add_convert_fusion.9), channel_id=1, source_target_pairs={{0,8},{2,10},{4,12},{6,14},{8,0},{10,2},{12,4},{14,6},{16,24},{18,... | collective-permute-start | bytes 1572872 | tf_op jit(solution)/shard_map/ppermute | solution.py:12
  469.4 74.1 %collective-permute-start.28 = (bf16[1,128,1024]{2,1,0:T(8,128)(2,1)S(1)}, bf16[1,128,1024]{2,1,0:T(8,128)(2,1)S(1)}, u32[]{:S(2)}, u32[]{:S(2)}) collective-permute-start(bf16[1,128,1024]{2,1,0:T(8,128)(2,1)S(1)} %add_convert_fusion.13), channel_id=1, source_target_pairs={{0,16},{2,18},{4,20},{6,22},{8,24},{10,26},{12,28},{14,30},{16,0},... | collective-permute-start | bytes 786440 | tf_op jit(solution)/shard_map/ppermute | solution.py:12
  545.1 1.4 collective-permute-start.29
  (33 other events, 131.9 us)
